TPU v7x, 512 devices: a whole 4x8x8 slice. The times are simulated.
512 devices in a mesh: gx: 4 (over y_lo, core), gy: 4 (over y_hi), gz: 32 (over z, x).
Axes of the slice: x: 4, y: 8 (y_hi: 4, y_lo: 2; y = y_hi * 2 + y_lo), z: 8, core: 2. Of those that a mesh axis runs over, the one named last changes fastest.
Arguments:
- density: float32 [512, 64, 4096], P('gz', 'gx', 'gy'), may hold values from 0.1 to 10
Outputs:
- details_one: float32 [7, 256, 32, 2048], P(None, 'gz', 'gx', 'gy')
- details_two: float32 [7, 128, 16, 1024], P(None, 'gz', 'gx', 'gy')
- details_three: float32 [7, 64, 8, 512], P(None, 'gz', 'gx', 'gy')
- approximation: float32 [64, 8, 512], P('gz', 'gx', 'gy')
All inputs are finite; a program needn't handle non-finite values.
Results may differ from a plain program's by a relative error of at most 0.00011.
Values sent between devices are 32-bit elements; how exact they have to be, the bound alone decides.
No kernel may reach another device: no remote copies, remote signals or barrier semaphores. Data moves between devices by JAX's collectives and lax.ppermute only.
A program may use at most 128 MiB of HBM per device.

v0:
```python
import jax
import jax.numpy as jnp
from jax import lax
from jax.sharding import PartitionSpec as P

ALPHA = -1.586134342
BETA = -0.05298011854
GAMMA = 0.8829110762
DELTA = 0.4435068522
ZETA = 1.149604398


def padded_2(x, sides, width):
    for axis, dim in sides:
        peers, length = (lax.axis_size(axis), x.shape[dim])
        up = [(i, (i + 1) % peers) for i in range(peers)]
        down = [(j, i) for i, j in up]
        last = lax.slice_in_dim(x, length - width, length, axis=dim)
        initial = lax.slice_in_dim(x, 0, width, axis=dim)
        before = lax.ppermute(last, axis, up)
        after = lax.ppermute(initial, axis, down)
        x = jnp.concatenate([before, x, after], axis=dim)
    return x


def cut(values, start, stop, dim):
    return lax.slice_in_dim(values, start, stop, 1, dim)


def lift_padded(padded, dim):
    length = padded.shape[dim]
    half = length // 2 - 4
    paired = padded.reshape(padded.shape[:dim] + (length // 2, 2) + padded.shape[dim + 1 :])
    evens = lax.index_in_dim(paired, 0, dim + 1, False)
    odds = lax.index_in_dim(paired, 1, dim + 1, False)
    first_d = cut(odds, 0, half + 3, dim) + ALPHA * (
        cut(evens, 0, half + 3, dim) + cut(evens, 1, half + 4, dim)
    )
    first_s = cut(evens, 1, half + 3, dim) + BETA * (
        cut(first_d, 0, half + 2, dim) + cut(first_d, 1, half + 3, dim)
    )
    second_d = cut(first_d, 1, half + 2, dim) + GAMMA * (
        cut(first_s, 0, half + 1, dim) + cut(first_s, 1, half + 2, dim)
    )
    second_s = cut(first_s, 1, half + 1, dim) + DELTA * (
        cut(second_d, 0, half, dim) + cut(second_d, 1, half + 1, dim)
    )
    lower = second_s * ZETA
    upper = cut(second_d, 1, half + 1, dim) / ZETA
    return jnp.concatenate([lower, upper], axis=0)


def pad_remote(data, dim):
    if dim == 2:
        return padded_2(data, (("gx", 2),), 4)
    if dim == 3:
        return padded_2(data, (("gy", 3),), 4)
    return padded_2(data, (("gz", 1),), 4)


def spread_level(data):
    for dim in (2, 3, 1):
        data = lift_padded(pad_remote(data, dim), dim)
    return data


def on_device(density):
    first = spread_level(density[None])
    details_one = first[1:]
    coarse = first[0:1]
    second = spread_level(coarse)
    third = spread_level(second[0:1])
    details_two = second[1:]
    details_three = third[1:]
    approximation = third[0]
    return (details_one, details_two, details_three, approximation)


def solution(mesh):
    return jax.shard_map(
        on_device,
        mesh=mesh,
        in_specs=(P("gz", "gx", "gy"),),
        out_specs=(
            P(None, "gz", "gx", "gy"),
            P(None, "gz", "gx", "gy"),
            P(None, "gz", "gx", "gy"),
            P("gz", "gx", "gy"),
        ),
        check_vma=False,
    )
```

profile of v0, /device:TPU:8, one launch (start us, length us, event | category | flops | bytes accessed | tf_op | source)
XLA Modules:
  0.0 150.3 jit_solution(17281420747032373268)
XLA Ops:
  0.6 1.8 %copy.127 = f32[16,16,1024]{2,0,1:T(8,128)S(1)} copy(f32[16,16,1024]{2,1,0:T(8,128)} %param.1) | data formatting | bytes 2097152 | tf_op args[0]
  2.5 1.9 %collective-permute-start = (f32[1,16,4,1024]{3,1,2,0:T(8,128)S(1)}, f32[1,16,4,1024]{3,1,2,0:T(8,128)S(1)}, u32[]{:S(2)}, u32[]{:S(2)}) collective-permute-start(f32[1,16,4,1024]{3,1,2,0:T(8,128)S(1)} %get-tuple-element.16), channel_id=1, source_target_pairs={{0,128},{128,256},{256,384},{384,0},{1,129},{129,257},{257,385},{3... | collective-permute-start | bytes 786440 | tf_op jit(solution)/shard_map/ppermute | solution.py:20
  4.4 3.6 %collective-permute-start.1 = (f32[1,16,4,1024]{3,1,2,0:T(8,128)S(1)}, f32[1,16,4,1024]{3,1,2,0:T(8,128)S(1)}, u32[]{:S(2)}, u32[]{:S(2)}) collective-permute-start(f32[1,16,4,1024]{3,1,2,0:T(8,128)S(1)} %get-tuple-element.17), channel_id=1, source_target_pairs={{128,0},{256,128},{384,256},{0,384},{129,1},{257,129},{385,257},{1... | collective-permute-start | bytes 786440 | tf_op jit(solution)/shard_map/ppermute | solution.py:21
  8.1 2.1 %collective-permute-done = f32[1,16,4,1024]{3,1,2,0:T(8,128)S(1)} collective-permute-done((f32[1,16,4,1024]{3,1,2,0:T(8,128)S(1)}, f32[1,16,4,1024]{3,1,2,0:T(8,128)S(1)}, u32[]{:S(2)}, u32[]{:S(2)}) %collective-permute-start) | collective-permute-done | bytes 262176 | tf_op jit(solution)/shard_map/ppermute | solution.py:20
  10.2 3.1 %collective-permute-done.1 = f32[1,16,4,1024]{3,1,2,0:T(8,128)S(1)} collective-permute-done((f32[1,16,4,1024]{3,1,2,0:T(8,128)S(1)}, f32[1,16,4,1024]{3,1,2,0:T(8,128)S(1)}, u32[]{:S(2)}, u32[]{:S(2)}) %collective-permute-start.1) | collective-permute-done | bytes 262176 | tf_op jit(solution)/shard_map/ppermute | solution.py:21
  15.0 3.9 %collective-permute-start.3 = (f32[2,16,8,4]{3,2,1,0:T(8,128)S(1)}, f32[2,16,8,4]{3,2,1,0:T(8,128)S(1)}, u32[]{:S(2)}, u32[]{:S(2)}) collective-permute-start(f32[2,16,8,4]{3,2,1,0:T(8,128)S(1)} %get-tuple-element.14), channel_id=1, source_target_pairs={{32,0},{64,32},{96,64},{0,96},{33,1},{65,33},{97,65},{1,97},{34,2}... | collective-permute-start | bytes 12296 | tf_op jit(solution)/shard_map/ppermute | solution.py:21
  18.9 2.8 %collective-permute-start.2 = (f32[2,16,8,4]{3,2,1,0:T(8,128)S(1)}, f32[2,16,8,4]{3,2,1,0:T(8,128)S(1)}, u32[]{:S(2)}, u32[]{:S(2)}) collective-permute-start(f32[2,16,8,4]{3,2,1,0:T(8,128)S(1)} %get-tuple-element.15), channel_id=1, source_target_pairs={{0,32},{32,64},{64,96},{96,0},{1,33},{33,65},{65,97},{97,1},{2,34}... | collective-permute-start | bytes 12296 | tf_op jit(solution)/shard_map/ppermute | solution.py:20
  21.7 2.0 %collective-permute-done.3 = f32[2,16,8,4]{3,2,1,0:T(8,128)S(1)} collective-permute-done((f32[2,16,8,4]{3,2,1,0:T(8,128)S(1)}, f32[2,16,8,4]{3,2,1,0:T(8,128)S(1)}, u32[]{:S(2)}, u32[]{:S(2)}) %collective-permute-start.3) | collective-permute-done | bytes 4128 | tf_op jit(solution)/shard_map/ppermute | solution.py:21
  23.7 7.2 %collective-permute-done.2 = f32[2,16,8,4]{3,2,1,0:T(8,128)S(1)} collective-permute-done((f32[2,16,8,4]{3,2,1,0:T(8,128)S(1)}, f32[2,16,8,4]{3,2,1,0:T(8,128)S(1)}, u32[]{:S(2)}, u32[]{:S(2)}) %collective-permute-start.2) | collective-permute-done | bytes 4128 | tf_op jit(solution)/shard_map/ppermute | solution.py:20
  31.0 0.8 concatenate.56
  31.8 5.1 %copy.97 = f32[2,16,8,1032]{1,2,3,0:T(8,128)} copy(f32[2,16,8,1032]{3,2,1,0:T(8,128)S(1)} %concatenate.56) | data formatting | bytes 2113536 | tf_op jit(solution)/shard_map/concatenate | solution.py:22
  36.9 7.3 %fusion.83 = (f32[2,16,8,516,1]{1,2,4,3,0:T(8,128)}, f32[2,16,8,516,1]{1,2,4,3,0:T(8,128)}) fusion(f32[2,16,8,516,2]{1,2,4,3,0:T(8,128)} %bitcast.55), kind=kLoop, calls=%fused_computation.166 | loop fusion | bytes 2113536 | tf_op jit(solution)/shard_map/slice | solution.py:35
  44.2 3.1 %copy.99 = f32[2,16,8,516,1]{3,2,1,0,4:T(8,128)S(1)} copy(f32[2,16,8,516,1]{1,2,4,3,0:T(8,128)} %get-tuple-element.4) | data formatting | bytes 1056768 | tf_op jit(solution)/shard_map/slice | solution.py:35
  47.3 3.1 %copy.115 = f32[2,16,8,516,1]{3,2,1,0,4:T(8,128)S(1)} copy(f32[2,16,8,516,1]{1,2,4,3,0:T(8,128)} %get-tuple-element.5) | data formatting | bytes 1056768
  50.6 0.4 fusion.9
  51.1 0.4 fusion.7
  51.9 4.2 %collective-permute-start.4 = (f32[4,4,8,512]{3,2,1,0:T(8,128)S(1)}, f32[4,4,8,512]{3,2,1,0:T(8,128)S(1)}, u32[]{:S(2)}, u32[]{:S(2)}) collective-permute-start(f32[4,4,8,512]{3,2,1,0:T(8,128)S(1)} %get-tuple-element.12), channel_id=1, source_target_pairs={{0,1},{1,2},{2,3},{3,4},{4,5},{5,6},{6,7},{7,8},{8,9},{9,10},{10,1... | collective-permute-start | bytes 786440 | tf_op jit(solution)/shard_map/ppermute | solution.py:20
  56.1 11.7 %collective-permute-start.5 = (f32[4,4,8,512]{3,2,1,0:T(8,128)S(1)}, f32[4,4,8,512]{3,2,1,0:T(8,128)S(1)}, u32[]{:S(2)}, u32[]{:S(2)}) collective-permute-start(f32[4,4,8,512]{3,2,1,0:T(8,128)S(1)} %get-tuple-element.13), channel_id=1, source_target_pairs={{1,0},{2,1},{3,2},{4,3},{5,4},{6,5},{7,6},{8,7},{9,8},{10,9},{11,1... | collective-permute-start | bytes 786440 | tf_op jit(solution)/shard_map/ppermute | solution.py:21
  67.8 4.6 %collective-permute-done.4 = f32[4,4,8,512]{3,2,1,0:T(8,128)S(1)} collective-permute-done((f32[4,4,8,512]{3,2,1,0:T(8,128)S(1)}, f32[4,4,8,512]{3,2,1,0:T(8,128)S(1)}, u32[]{:S(2)}, u32[]{:S(2)}) %collective-permute-start.4) | collective-permute-done | bytes 262176 | tf_op jit(solution)/shard_map/ppermute | solution.py:20
  72.4 1.2 collective-permute-done.5
  74.3 1.0 fusion.20
  75.3 1.9 %collective-permute-start.6 = (f32[1,8,4,512]{3,2,1,0:T(4,128)S(1)}, f32[1,8,4,512]{3,2,1,0:T(4,128)S(1)}, u32[]{:S(2)}, u32[]{:S(2)}) collective-permute-start(f32[1,8,4,512]{3,2,1,0:T(4,128)S(1)} %get-tuple-element.26), channel_id=1, source_target_pairs={{0,128},{128,256},{256,384},{384,0},{1,129},{129,257},{257,385},{3... | collective-permute-start | bytes 196616 | tf_op jit(solution)/shard_map/ppermute | solution.py:20
  77.2 3.6 %collective-permute-start.7 = (f32[1,8,4,512]{3,2,1,0:T(4,128)S(1)}, f32[1,8,4,512]{3,2,1,0:T(4,128)S(1)}, u32[]{:S(2)}, u32[]{:S(2)}) collective-permute-start(f32[1,8,4,512]{3,2,1,0:T(4,128)S(1)} %get-tuple-element.27), channel_id=1, source_target_pairs={{128,0},{256,128},{384,256},{0,384},{129,1},{257,129},{385,257},{1... | collective-permute-start | bytes 196616 | tf_op jit(solution)/shard_map/ppermute | solution.py:21
  80.9 1.8 %collective-permute-done.7 = f32[1,8,4,512]{3,2,1,0:T(4,128)S(1)} collective-permute-done((f32[1,8,4,512]{3,2,1,0:T(4,128)S(1)}, f32[1,8,4,512]{3,2,1,0:T(4,128)S(1)}, u32[]{:S(2)}, u32[]{:S(2)}) %collective-permute-start.7) | collective-permute-done | bytes 65568 | tf_op jit(solution)/shard_map/ppermute | solution.py:21
  83.6 1.9 %collective-permute-start.8 = (f32[2,8,4,4]{3,1,2,0:T(8,128)S(1)}, f32[2,8,4,4]{3,1,2,0:T(8,128)S(1)}, u32[]{:S(2)}, u32[]{:S(2)}) collective-permute-start(f32[2,8,4,4]{3,1,2,0:T(8,128)S(1)} %get-tuple-element.34), channel_id=1, source_target_pairs={{0,32},{32,64},{64,96},{96,0},{1,33},{33,65},{65,97},{97,1},{2,34}... | collective-permute-start | bytes 3080 | tf_op jit(solution)/shard_map/ppermute | solution.py:20
  85.5 6.0 %collective-permute-start.9 = (f32[2,8,4,4]{3,1,2,0:T(8,128)S(1)}, f32[2,8,4,4]{3,1,2,0:T(8,128)S(1)}, u32[]{:S(2)}, u32[]{:S(2)}) collective-permute-start(f32[2,8,4,4]{3,1,2,0:T(8,128)S(1)} %get-tuple-element.35), channel_id=1, source_target_pairs={{32,0},{64,32},{96,64},{0,96},{33,1},{65,33},{97,65},{1,97},{34,2}... | collective-permute-start | bytes 3080 | tf_op jit(solution)/shard_map/ppermute | solution.py:21
  91.5 1.6 %collective-permute-done.9 = f32[2,8,4,4]{3,1,2,0:T(8,128)S(1)} collective-permute-done((f32[2,8,4,4]{3,1,2,0:T(8,128)S(1)}, f32[2,8,4,4]{3,1,2,0:T(8,128)S(1)}, u32[]{:S(2)}, u32[]{:S(2)}) %collective-permute-start.9) | collective-permute-done | bytes 1056 | tf_op jit(solution)/shard_map/ppermute | solution.py:21
  93.2 0.6 copy.103
  93.8 2.7 %fusion.84 = (f32[2,8,4,260,1]{1,4,3,2,0:T(1,128)}, f32[2,8,4,260,1]{1,4,3,2,0:T(1,128)S(1)}) fusion(f32[2,8,4,260,2]{1,4,3,2,0:T(2,128)S(1)} %bitcast.58), kind=kLoop, calls=%fused_computation.167 | loop fusion | bytes 266240 | tf_op jit(solution)/shard_map/slice | solution.py:35
  96.5 2.3 %copy.105 = f32[2,8,4,260,1]{3,1,4,2,0:T(8,128)S(1)} copy(f32[2,8,4,260,1]{1,4,3,2,0:T(1,128)} %get-tuple-element.6) | data formatting | bytes 133120 | tf_op jit(solution)/shard_map/slice | solution.py:35
  98.8 0.6 copy.104
  99.9 1.9 %collective-permute-start.10 = (f32[4,4,4,256]{3,1,2,0:T(4,128)S(1)}, f32[4,4,4,256]{3,1,2,0:T(4,128)S(1)}, u32[]{:S(2)}, u32[]{:S(2)}) collective-permute-start(f32[4,4,4,256]{3,1,2,0:T(4,128)S(1)} %get-tuple-element.32), channel_id=1, source_target_pairs={{0,1},{1,2},{2,3},{3,4},{4,5},{5,6},{6,7},{7,8},{8,9},{9,10},{10,1... | collective-permute-start | bytes 196616 | tf_op jit(solution)/shard_map/ppermute | solution.py:20
  101.9 7.7 %collective-permute-start.11 = (f32[4,4,4,256]{3,1,2,0:T(4,128)S(1)}, f32[4,4,4,256]{3,1,2,0:T(4,128)S(1)}, u32[]{:S(2)}, u32[]{:S(2)}) collective-permute-start(f32[4,4,4,256]{3,1,2,0:T(4,128)S(1)} %get-tuple-element.33), channel_id=1, source_target_pairs={{1,0},{2,1},{3,2},{4,3},{5,4},{6,5},{7,6},{8,7},{9,8},{10,9},{11,1... | collective-permute-start | bytes 196616 | tf_op jit(solution)/shard_map/ppermute | solution.py:21
  109.9 1.6 %collective-permute-done.11 = f32[4,4,4,256]{3,1,2,0:T(4,128)S(1)} collective-permute-done((f32[4,4,4,256]{3,1,2,0:T(4,128)S(1)}, f32[4,4,4,256]{3,1,2,0:T(4,128)S(1)}, u32[]{:S(2)}, u32[]{:S(2)}) %collective-permute-start.11) | collective-permute-done | bytes 65568 | tf_op jit(solution)/shard_map/ppermute | solution.py:21
  112.0 1.9 %collective-permute-start.13 = (f32[1,4,4,256]{3,2,1,0:T(4,128)S(1)}, f32[1,4,4,256]{3,2,1,0:T(4,128)S(1)}, u32[]{:S(2)}, u32[]{:S(2)}) collective-permute-start(f32[1,4,4,256]{3,2,1,0:T(4,128)S(1)} %slice.688), channel_id=1, source_target_pairs={{128,0},{256,128},{384,256},{0,384},{129,1},{257,129},{385,257},{1... | collective-permute-start | bytes 49160 | tf_op jit(solution)/shard_map/ppermute | solution.py:21
  113.9 2.4 %collective-permute-start.12 = (f32[1,4,4,256]{3,2,1,0:T(4,128)S(1)}, f32[1,4,4,256]{3,2,1,0:T(4,128)S(1)}, u32[]{:S(2)}, u32[]{:S(2)}) collective-permute-start(f32[1,4,4,256]{3,2,1,0:T(4,128)S(1)} %slice.688), channel_id=1, source_target_pairs={{0,128},{128,256},{256,384},{384,0},{1,129},{129,257},{257,385},{3... | collective-permute-start | bytes 49160 | tf_op jit(solution)/shard_map/ppermute | solution.py:20
  116.3 2.6 %collective-permute-done.12 = f32[1,4,4,256]{3,2,1,0:T(4,128)S(1)} collective-permute-done((f32[1,4,4,256]{3,2,1,0:T(4,128)S(1)}, f32[1,4,4,256]{3,2,1,0:T(4,128)S(1)}, u32[]{:S(2)}, u32[]{:S(2)}) %collective-permute-start.12) | collective-permute-done | bytes 16416 | tf_op jit(solution)/shard_map/ppermute | solution.py:20
  119.2 5.2 %collective-permute-start.14 = (f32[2,4,2,4]{3,1,2,0:T(4,128)S(1)}, f32[2,4,2,4]{3,1,2,0:T(4,128)S(1)}, u32[]{:S(2)}, u32[]{:S(2)}) collective-permute-start(f32[2,4,2,4]{3,1,2,0:T(4,128)S(1)} %get-tuple-element.48), channel_id=1, source_target_pairs={{0,32},{32,64},{64,96},{96,0},{1,33},{33,65},{65,97},{97,1},{2,34}... | collective-permute-start | bytes 776 | tf_op jit(solution)/shard_map/ppermute | solution.py:20
  124.4 3.1 %collective-permute-start.15 = (f32[2,4,2,4]{3,1,2,0:T(4,128)S(1)}, f32[2,4,2,4]{3,1,2,0:T(4,128)S(1)}, u32[]{:S(2)}, u32[]{:S(2)}) collective-permute-start(f32[2,4,2,4]{3,1,2,0:T(4,128)S(1)} %get-tuple-element.49), channel_id=1, source_target_pairs={{32,0},{64,32},{96,64},{0,96},{33,1},{65,33},{97,65},{1,97},{34,2}... | collective-permute-start | bytes 776 | tf_op jit(solution)/shard_map/ppermute | solution.py:21
  127.5 1.0 pad_maximum_fusion.2
  128.5 2.3 %collective-permute-done.15 = f32[2,4,2,4]{3,1,2,0:T(4,128)S(1)} collective-permute-done((f32[2,4,2,4]{3,1,2,0:T(4,128)S(1)}, f32[2,4,2,4]{3,1,2,0:T(4,128)S(1)}, u32[]{:S(2)}, u32[]{:S(2)}) %collective-permute-start.15) | collective-permute-done | bytes 288 | tf_op jit(solution)/shard_map/ppermute | solution.py:21
  131.1 0.4 fusion.87
  132.4 7.6 %collective-permute-start.17 = (f32[4,4,2,128]{3,2,1,0:T(2,128)S(1)}, f32[4,4,2,128]{3,2,1,0:T(2,128)S(1)}, u32[]{:S(2)}, u32[]{:S(2)}) collective-permute-start(f32[4,4,2,128]{3,2,1,0:T(2,128)S(1)} %pad_maximum_fusion.15), channel_id=1, source_target_pairs={{1,0},{2,1},{3,2},{4,3},{5,4},{6,5},{7,6},{8,7},{9,8},{10,9},{11,1... | collective-permute-start | bytes 49160 | tf_op jit(solution)/shard_map/ppermute | solution.py:21
  140.0 1.9 %collective-permute-start.16 = (f32[4,4,2,128]{3,2,1,0:T(2,128)S(1)}, f32[4,4,2,128]{3,2,1,0:T(2,128)S(1)}, u32[]{:S(2)}, u32[]{:S(2)}) collective-permute-start(f32[4,4,2,128]{3,2,1,0:T(2,128)S(1)} %pad_maximum_fusion.15), channel_id=1, source_target_pairs={{0,1},{1,2},{2,3},{3,4},{4,5},{5,6},{6,7},{7,8},{8,9},{9,10},{10,1... | collective-permute-start | bytes 49160 | tf_op jit(solution)/shard_map/ppermute | solution.py:20
  141.9 0.7 pad_maximum_fusion.8
  142.6 6.3 %collective-permute-done.16 = f32[4,4,2,128]{3,2,1,0:T(2,128)S(1)} collective-permute-done((f32[4,4,2,128]{3,2,1,0:T(2,128)S(1)}, f32[4,4,2,128]{3,2,1,0:T(2,128)S(1)}, u32[]{:S(2)}, u32[]{:S(2)}) %collective-permute-start.16) | collective-permute-done | bytes 16416 | tf_op jit(solution)/shard_map/ppermute | solution.py:20
  149.1 0.6 slice_bitcast_fusion.10
  149.7 0.6 pad_maximum_fusion.16
  (78 shorter events, 6.4 us)
Async XLA Ops:
  2.5 7.7 %collective-permute-start = (f32[1,16,4,1024]{3,1,2,0:T(8,128)S(1)}, f32[1,16,4,1024]{3,1,2,0:T(8,128)S(1)}, u32[]{:S(2)}, u32[]{:S(2)}) collective-permute-start(f32[1,16,4,1024]{3,1,2,0:T(8,128)S(1)} %get-tuple-element.16), channel_id=1, source_target_pairs={{0,128},{128,256},{256,384},{384,0},{1,129},{129,257},{257,385},{3... | collective-permute-start | bytes 786440 | tf_op jit(solution)/shard_map/ppermute | solution.py:20
  4.4 8.9 %collective-permute-start.1 = (f32[1,16,4,1024]{3,1,2,0:T(8,128)S(1)}, f32[1,16,4,1024]{3,1,2,0:T(8,128)S(1)}, u32[]{:S(2)}, u32[]{:S(2)}) collective-permute-start(f32[1,16,4,1024]{3,1,2,0:T(8,128)S(1)} %get-tuple-element.17), channel_id=1, source_target_pairs={{128,0},{256,128},{384,256},{0,384},{129,1},{257,129},{385,257},{1... | collective-permute-start | bytes 786440 | tf_op jit(solution)/shard_map/ppermute | solution.py:21
  15.0 8.8 %collective-permute-start.3 = (f32[2,16,8,4]{3,2,1,0:T(8,128)S(1)}, f32[2,16,8,4]{3,2,1,0:T(8,128)S(1)}, u32[]{:S(2)}, u32[]{:S(2)}) collective-permute-start(f32[2,16,8,4]{3,2,1,0:T(8,128)S(1)} %get-tuple-element.14), channel_id=1, source_target_pairs={{32,0},{64,32},{96,64},{0,96},{33,1},{65,33},{97,65},{1,97},{34,2}... | collective-permute-start | bytes 12296 | tf_op jit(solution)/shard_map/ppermute | solution.py:21
  18.9 12.1 %collective-permute-start.2 = (f32[2,16,8,4]{3,2,1,0:T(8,128)S(1)}, f32[2,16,8,4]{3,2,1,0:T(8,128)S(1)}, u32[]{:S(2)}, u32[]{:S(2)}) collective-permute-start(f32[2,16,8,4]{3,2,1,0:T(8,128)S(1)} %get-tuple-element.15), channel_id=1, source_target_pairs={{0,32},{32,64},{64,96},{96,0},{1,33},{33,65},{65,97},{97,1},{2,34}... | collective-permute-start | bytes 12296 | tf_op jit(solution)/shard_map/ppermute | solution.py:20
  51.9 20.5 %collective-permute-start.4 = (f32[4,4,8,512]{3,2,1,0:T(8,128)S(1)}, f32[4,4,8,512]{3,2,1,0:T(8,128)S(1)}, u32[]{:S(2)}, u32[]{:S(2)}) collective-permute-start(f32[4,4,8,512]{3,2,1,0:T(8,128)S(1)} %get-tuple-element.12), channel_id=1, source_target_pairs={{0,1},{1,2},{2,3},{3,4},{4,5},{5,6},{6,7},{7,8},{8,9},{9,10},{10,1... | collective-permute-start | bytes 786440 | tf_op jit(solution)/shard_map/ppermute | solution.py:20
  56.1 17.5 %collective-permute-start.5 = (f32[4,4,8,512]{3,2,1,0:T(8,128)S(1)}, f32[4,4,8,512]{3,2,1,0:T(8,128)S(1)}, u32[]{:S(2)}, u32[]{:S(2)}) collective-permute-start(f32[4,4,8,512]{3,2,1,0:T(8,128)S(1)} %get-tuple-element.13), channel_id=1, source_target_pairs={{1,0},{2,1},{3,2},{4,3},{5,4},{6,5},{7,6},{8,7},{9,8},{10,9},{11,1... | collective-permute-start | bytes 786440 | tf_op jit(solution)/shard_map/ppermute | solution.py:21
  75.3 5.6 %copy-start = (f32[4,8,8,512]{3,2,1,0:T(8,128)}, f32[4,8,8,512]{3,2,1,0:T(8,128)S(1)}, u32[]{:S(2)}) copy-start(f32[4,8,8,512]{3,2,1,0:T(8,128)S(1)} %get-tuple-element.20) | copy-start | bytes 1572868
  75.3 5.6 %collective-permute-start.6 = (f32[1,8,4,512]{3,2,1,0:T(4,128)S(1)}, f32[1,8,4,512]{3,2,1,0:T(4,128)S(1)}, u32[]{:S(2)}, u32[]{:S(2)}) collective-permute-start(f32[1,8,4,512]{3,2,1,0:T(4,128)S(1)} %get-tuple-element.26), channel_id=1, source_target_pairs={{0,128},{128,256},{256,384},{384,0},{1,129},{129,257},{257,385},{3... | collective-permute-start | bytes 196616 | tf_op jit(solution)/shard_map/ppermute | solution.py:20
  77.2 5.5 %collective-permute-start.7 = (f32[1,8,4,512]{3,2,1,0:T(4,128)S(1)}, f32[1,8,4,512]{3,2,1,0:T(4,128)S(1)}, u32[]{:S(2)}, u32[]{:S(2)}) collective-permute-start(f32[1,8,4,512]{3,2,1,0:T(4,128)S(1)} %get-tuple-element.27), channel_id=1, source_target_pairs={{128,0},{256,128},{384,256},{0,384},{129,1},{257,129},{385,257},{1... | collective-permute-start | bytes 196616 | tf_op jit(solution)/shard_map/ppermute | solution.py:21
  83.6 8.0 %collective-permute-start.8 = (f32[2,8,4,4]{3,1,2,0:T(8,128)S(1)}, f32[2,8,4,4]{3,1,2,0:T(8,128)S(1)}, u32[]{:S(2)}, u32[]{:S(2)}) collective-permute-start(f32[2,8,4,4]{3,1,2,0:T(8,128)S(1)} %get-tuple-element.34), channel_id=1, source_target_pairs={{0,32},{32,64},{64,96},{96,0},{1,33},{33,65},{65,97},{97,1},{2,34}... | collective-permute-start | bytes 3080 | tf_op jit(solution)/shard_map/ppermute | solution.py:20
  85.5 7.6 %collective-permute-start.9 = (f32[2,8,4,4]{3,1,2,0:T(8,128)S(1)}, f32[2,8,4,4]{3,1,2,0:T(8,128)S(1)}, u32[]{:S(2)}, u32[]{:S(2)}) collective-permute-start(f32[2,8,4,4]{3,1,2,0:T(8,128)S(1)} %get-tuple-element.35), channel_id=1, source_target_pairs={{32,0},{64,32},{96,64},{0,96},{33,1},{65,33},{97,65},{1,97},{34,2}... | collective-permute-start | bytes 3080 | tf_op jit(solution)/shard_map/ppermute | solution.py:21
  99.9 9.9 %collective-permute-start.10 = (f32[4,4,4,256]{3,1,2,0:T(4,128)S(1)}, f32[4,4,4,256]{3,1,2,0:T(4,128)S(1)}, u32[]{:S(2)}, u32[]{:S(2)}) collective-permute-start(f32[4,4,4,256]{3,1,2,0:T(4,128)S(1)} %get-tuple-element.32), channel_id=1, source_target_pairs={{0,1},{1,2},{2,3},{3,4},{4,5},{5,6},{6,7},{7,8},{8,9},{9,10},{10,1... | collective-permute-start | bytes 196616 | tf_op jit(solution)/shard_map/ppermute | solution.py:20
  101.9 9.6 %collective-permute-start.11 = (f32[4,4,4,256]{3,1,2,0:T(4,128)S(1)}, f32[4,4,4,256]{3,1,2,0:T(4,128)S(1)}, u32[]{:S(2)}, u32[]{:S(2)}) collective-permute-start(f32[4,4,4,256]{3,1,2,0:T(4,128)S(1)} %get-tuple-element.33), channel_id=1, source_target_pairs={{1,0},{2,1},{3,2},{4,3},{5,4},{6,5},{7,6},{8,7},{9,8},{10,9},{11,1... | collective-permute-start | bytes 196616 | tf_op jit(solution)/shard_map/ppermute | solution.py:21
  111.5 15.9 %copy-start.1 = (f32[4,8,8,512]{3,2,1,0:T(8,128)S(1)}, f32[4,8,8,512]{3,2,1,0:T(8,128)}, u32[]{:S(2)}) copy-start(f32[4,8,8,512]{3,2,1,0:T(8,128)} %copy-done) | copy-start | bytes 1572868
  111.5 15.9 %copy-start.2 = (f32[4,8,8,512]{3,2,1,0:T(8,128)S(1)}, f32[4,8,8,512]{3,2,1,0:T(8,128)}, u32[]{:S(2)}) copy-start(f32[4,8,8,512]{3,2,1,0:T(8,128)} %get-tuple-element.21) | copy-start | bytes 1572868
  112.0 4.3 %collective-permute-start.13 = (f32[1,4,4,256]{3,2,1,0:T(4,128)S(1)}, f32[1,4,4,256]{3,2,1,0:T(4,128)S(1)}, u32[]{:S(2)}, u32[]{:S(2)}) collective-permute-start(f32[1,4,4,256]{3,2,1,0:T(4,128)S(1)} %slice.688), channel_id=1, source_target_pairs={{128,0},{256,128},{384,256},{0,384},{129,1},{257,129},{385,257},{1... | collective-permute-start | bytes 49160 | tf_op jit(solution)/shard_map/ppermute | solution.py:21
  113.9 5.1 %collective-permute-start.12 = (f32[1,4,4,256]{3,2,1,0:T(4,128)S(1)}, f32[1,4,4,256]{3,2,1,0:T(4,128)S(1)}, u32[]{:S(2)}, u32[]{:S(2)}) collective-permute-start(f32[1,4,4,256]{3,2,1,0:T(4,128)S(1)} %slice.688), channel_id=1, source_target_pairs={{0,128},{128,256},{256,384},{384,0},{1,129},{129,257},{257,385},{3... | collective-permute-start | bytes 49160 | tf_op jit(solution)/shard_map/ppermute | solution.py:20
  119.2 9.3 %collective-permute-start.14 = (f32[2,4,2,4]{3,1,2,0:T(4,128)S(1)}, f32[2,4,2,4]{3,1,2,0:T(4,128)S(1)}, u32[]{:S(2)}, u32[]{:S(2)}) collective-permute-start(f32[2,4,2,4]{3,1,2,0:T(4,128)S(1)} %get-tuple-element.48), channel_id=1, source_target_pairs={{0,32},{32,64},{64,96},{96,0},{1,33},{33,65},{65,97},{97,1},{2,34}... | collective-permute-start | bytes 776 | tf_op jit(solution)/shard_map/ppermute | solution.py:20
  124.4 6.4 %collective-permute-start.15 = (f32[2,4,2,4]{3,1,2,0:T(4,128)S(1)}, f32[2,4,2,4]{3,1,2,0:T(4,128)S(1)}, u32[]{:S(2)}, u32[]{:S(2)}) collective-permute-start(f32[2,4,2,4]{3,1,2,0:T(4,128)S(1)} %get-tuple-element.49), channel_id=1, source_target_pairs={{32,0},{64,32},{96,64},{0,96},{33,1},{65,33},{97,65},{1,97},{34,2}... | collective-permute-start | bytes 776 | tf_op jit(solution)/shard_map/ppermute | solution.py:21
  132.4 10.2 %collective-permute-start.17 = (f32[4,4,2,128]{3,2,1,0:T(2,128)S(1)}, f32[4,4,2,128]{3,2,1,0:T(2,128)S(1)}, u32[]{:S(2)}, u32[]{:S(2)}) collective-permute-start(f32[4,4,2,128]{3,2,1,0:T(2,128)S(1)} %pad_maximum_fusion.15), channel_id=1, source_target_pairs={{1,0},{2,1},{3,2},{4,3},{5,4},{6,5},{7,6},{8,7},{9,8},{10,9},{11,1... | collective-permute-start | bytes 49160 | tf_op jit(solution)/shard_map/ppermute | solution.py:21
  140.0 9.0 %collective-permute-start.16 = (f32[4,4,2,128]{3,2,1,0:T(2,128)S(1)}, f32[4,4,2,128]{3,2,1,0:T(2,128)S(1)}, u32[]{:S(2)}, u32[]{:S(2)}) collective-permute-start(f32[4,4,2,128]{3,2,1,0:T(2,128)S(1)} %pad_maximum_fusion.15), channel_id=1, source_target_pairs={{0,1},{1,2},{2,3},{3,4},{4,5},{5,6},{6,7},{7,8},{8,9},{9,10},{10,1... | collective-permute-start | bytes 49160 | tf_op jit(solution)/shard_map/ppermute | solution.py:20
where the time goes:
time: 151 us; the launch traced here: 150 us
  starting transfers between devices  73.4 us (49%)
  waiting for transfers between devices  36.9 us (24%)
  local copies, waits for them, and re-layouts  31 us (21%)
  other arithmetic  7.61 us (5%)
    ppermute x9, starting transfers between devices, padded_2(): after = lax.ppermute(initial, axis, down)  49.2 us
    ppermute x9, starting transfers between devices, padded_2(): before = lax.ppermute(last, axis, up)  24.2 us
    ppermute x9, waiting for transfers between devices, padded_2(): before = lax.ppermute(last, axis, up)  23.3 us
    slice x7, local copies, waits for them, and re-layouts, lift_padded(): odds = lax.index_in_dim(paired, 1, dim + 1, False)  16.3 us
    ppermute x9, waiting for transfers between devices, padded_2(): after = lax.ppermute(initial, axis, down)  13.6 us
    concatenate x6, local copies, waits for them, and re-layouts, padded_2(): x = jnp.concatenate([before, x, after], axis=dim)  6.99 us
    unnamed x9, local copies, waits for them, and re-layouts  5.24 us
  transfers between devices with their start and end apart: 18, of which 13 were waited for; matrix products, arithmetic and copies ran while one was open for 1% of the time, Pallas kernels for 0%

commit v1 on v0

v1 whole, which is shorter than its diff:
```python
import functools

import jax
import jax.numpy as jnp
import numpy as np
from jax import lax
from jax.experimental import pallas as pl
from jax.experimental.pallas import tpu as pltpu
from jax.sharding import PartitionSpec as P

ALPHA = -1.586134342
BETA = -0.05298011854
GAMMA = 0.8829110762
DELTA = 0.4435068522
ZETA = 1.149604398

N = 16
F32 = jnp.float32


def plus(a, b):
    if a is None:
        return b
    return a if b is None else a + b


def times(c, a):
    return None if a is None else c * a


class Level:
    def __init__(self, line):
        self.line = line
        self.memo = {}

    def get(self, name, i):
        if (name, i) not in self.memo:
            self.memo[name, i] = getattr(self, name)(i)
        return self.memo[name, i]

    def s0(self, i):
        return self.line(2 * i)

    def d0(self, i):
        return self.line(2 * i + 1)

    def d1(self, i):
        return plus(self.get("d0", i), times(ALPHA, plus(self.get("s0", i), self.get("s0", i + 1))))

    def s1(self, i):
        return plus(self.get("s0", i), times(BETA, plus(self.get("d1", i - 1), self.get("d1", i))))

    def d2(self, i):
        return plus(self.get("d1", i), times(GAMMA, plus(self.get("s1", i), self.get("s1", i + 1))))

    def s2(self, i):
        return plus(self.get("s1", i), times(DELTA, plus(self.get("d2", i - 1), self.get("d2", i))))

    def low(self, i):
        return times(ZETA, self.get("s2", i))

    def high(self, i):
        return times(1.0 / ZETA, self.get("d2", i))


def block_levels(rows, count):
    line = lambda i: rows[i] if 0 <= i < N else None
    for _ in range(count):
        level = Level(line)
        line = functools.partial(level.get, "low")
    return level


BANDS = ("low", "high")


def own_count(count):
    return N >> count


def spill_matrices(count):
    n = own_count(count)
    level = block_levels(list(np.eye(N)), count)
    zero = np.zeros(N)

    def at(band, i):
        value = level.get(band, i)
        return zero if value is None else value

    return {
        offset: np.stack([at(band, offset * n + i) for band in BANDS for i in range(n)])
        for offset in (-2, -1, 1, 2)
    }


def factor(matrix):
    picked, rest = [], matrix.copy()
    scale = np.abs(matrix).max()
    while scale > 0 and np.abs(rest).max() > 1e-10 * scale:
        row = int(np.argmax((rest**2).sum(1)))
        picked.append(row)
        q = rest[row] / np.linalg.norm(rest[row])
        rest = rest - np.outer(rest @ q, q)
    picked.sort()
    if not picked:
        return [], None
    coefs = np.linalg.lstsq(matrix[picked].T, matrix.T, rcond=None)[0].T
    coefs[np.abs(coefs) < 1e-9] = 0.0
    coefs[np.abs(coefs - 1.0) < 1e-9] = 1.0
    return picked, coefs


PLAN = {count: {o: factor(m) for o, m in spill_matrices(count).items()} for count in (1, 2, 3)}
TILES = {1: 8, 2: 4, 3: 2}


def sent(level, count, offset):
    n = own_count(count)
    return [level.get(BANDS[row // n], offset * n + row % n) for row in PLAN[count][offset][0]]


def added(count, offset, row, lines):
    coefs = PLAN[count][offset][1][row]
    total = None
    for c, line in zip(coefs, lines):
        if c != 0.0:
            total = plus(total, line() if c == 1.0 else times(float(c), line()))
    return total


def message_places(height, offsets, counts):
    places, at = {}, 0
    for offset in offsets:
        for count in counts:
            for k in range(len(PLAN[count][offset][0])):
                for t in range(TILES[count]):
                    places[count, offset, k, t] = at
                    at += height[count]
    return places, at


X_HEIGHT = {1: N, 2: N, 3: N}
Z_HEIGHT = {1: 16, 2: 8, 3: 4}
ALL = (1, 2, 3)
X_UP = message_places(X_HEIGHT, (1,), ALL)
X_DOWN = message_places(X_HEIGHT, (-1,), ALL)
X_FAR = message_places(X_HEIGHT, (2, -2), (3,))
Z_UP = message_places(Z_HEIGHT, (1,), ALL)
Z_DOWN = message_places(Z_HEIGHT, (-1,), ALL)
Z_UP2 = message_places(Z_HEIGHT, (2,), (3,))
Z_DOWN2 = message_places(Z_HEIGHT, (-2,), (3,))


def pack_kernel(first_ref, last_ref, to_down_ref, to_up_ref):
    lane = lax.broadcasted_iota(jnp.int32, (64, 128), 1)
    down = up = jnp.zeros((64, 128), F32)
    for g in range(4):
        mine = (lane >= 32 * g) & (lane < 32 * g + 32)
        rows = pl.ds(64 * g, 64)
        a, b = first_ref[rows, :], last_ref[rows, :]
        a = pltpu.roll(a, 32 * g, 1) if g else a
        b = pltpu.roll(b, (32 * g + 32) % 128, 1) if (32 * g + 32) % 128 else b
        down = jnp.where(mine, a, down)
        up = jnp.where(mine, b, up)
    to_down_ref[...] = down
    to_up_ref[...] = up


def split_dot(x, selection):
    hi = x.astype(jnp.bfloat16)
    rest = x - hi.astype(F32)
    mid = rest.astype(jnp.bfloat16)
    lo = (rest - mid.astype(F32)).astype(jnp.bfloat16)
    dot = functools.partial(jnp.dot, preferred_element_type=F32)
    return (dot(lo, selection) + dot(mid, selection)) + dot(hi, selection)


def y_level(source, tiles, halo, even, odd, out, low_halo):
    half = tiles // 2
    width = half * 128 + 128
    i = lax.broadcasted_iota(jnp.int32, (256, 256), 0)
    j = lax.broadcasted_iota(jnp.int32, (256, 256), 1)
    pick = (i == 2 * (j % 128) + j // 128).astype(jnp.bfloat16)
    i = lax.broadcasted_iota(jnp.int32, (128, 256), 0)
    j = lax.broadcasted_iota(jnp.int32, (128, 256), 1)
    pick_halo = (i == (2 * (j % 128) + j // 128) % 128).astype(jnp.bfloat16)
    for t in range(half):
        both = split_dot(source(t), pick)
        even[:, pl.ds(128 * t, 128)] = both[:, :128]
        odd[:, pl.ds(128 * t, 128)] = both[:, 128:]
    both = split_dot(halo(), pick_halo)
    even[:, pl.ds(128 * half, 128)] = both[:, :128]
    odd[:, pl.ds(128 * half, 128)] = both[:, 128:]
    chunk = 16
    for r in range(0, 256, chunk):
        rows = pl.ds(r, chunk)
        s, d = even[rows, :width], odd[rows, :width]
        ahead = lambda v: pltpu.roll(v, width - 1, 1)
        behind = lambda v: pltpu.roll(v, 1, 1)
        d = d + ALPHA * (s + ahead(s))
        s = s + BETA * (behind(d) + d)
        d = d + GAMMA * (s + ahead(s))
        s = s + DELTA * (behind(d) + d)
        for t in range(half):
            out[t, rows, :] = s[:, 128 * t : 128 * t + 128] * ZETA
            out[half + t, rows, :] = d[:, 128 * t : 128 * t + 128] * (1.0 / ZETA)
        if low_halo is not None:
            low_halo[rows, :] = s[:, 128 * half :] * ZETA


def put(ref, places, key, value):
    ref[pl.ds(places[key], value.shape[0]), :] = value


def y_kernel(x_ref, above_ref, below_ref, o1, o2, o3, up_ref, down_ref, far_ref, even, odd, halo, halo2, g1, g2, g3):
    lane = lax.broadcasted_iota(jnp.int32, (64, 128), 1)
    for g in range(4):
        a, b = above_ref[...], below_ref[...]
        a = pltpu.roll(a, 128 - 32 * g, 1) if g else a
        b = pltpu.roll(b, 96 - 32 * g, 1) if g < 3 else b
        halo[pl.ds(64 * g, 64), :] = jnp.where(lane < 32, a, jnp.where(lane >= 96, b, 0.0))

    def pair(g):
        return lambda t: jnp.concatenate([g[2 * t], g[2 * t + 1]], axis=1)

    y_level(lambda t: x_ref[:, pl.ds(256 * t, 256)], 8, lambda: halo[...], even, odd, g1, halo2)
    y_level(pair(g1), 4, lambda: halo2[...], even, odd, g2, halo)
    y_level(pair(g2), 2, lambda: halo[...], even, odd, g3, None)

    for count, g, o in ((1, g1, o1), (2, g2, o2), (3, g3, o3)):
        n = own_count(count)
        for t in range(TILES[count]):
            rows = [g[t, pl.ds(x, N, stride=N), :] for x in range(N)]
            level = block_levels(rows, count)
            for k, v in enumerate(sent(level, count, 1)):
                put(up_ref, X_UP[0], (count, 1, k, t), v)
            for k, v in enumerate(sent(level, count, -1)):
                put(down_ref, X_DOWN[0], (count, -1, k, t), v)
            if count == 3:
                for offset in (2, -2):
                    for k, v in enumerate(sent(level, count, offset)):
                        put(far_ref, X_FAR[0], (count, offset, k, t), v)
            for b, band in enumerate(BANDS):
                for i in range(n):
                    o[t, pl.ds((b * n + i) * N, N), :] = level.get(band, i)


def received(count, row, t, height, sources):
    total = None
    for offset, places, ref in sources:
        if not PLAN[count][offset][0]:
            continue

        def line(k, offset=offset, places=places, ref=ref):
            return ref[pl.ds(places[count, offset, k, t], height), :]

        lines = [functools.partial(line, k) for k in range(len(PLAN[count][offset][0]))]
        total = plus(total, added(count, offset, row, lines))
    return total


def x_kernel(i1, i2, i3, up_in, down_in, far_in, o1, o2, o3, up_ref, down_ref, up2_ref, down2_ref, g1, g2, g3):
    near = [(1, X_UP[0], up_in), (-1, X_DOWN[0], down_in)]
    far = [(2, X_FAR[0], far_in), (-2, X_FAR[0], far_in)]
    for count, own, g, o in ((1, i1, g1, o1), (2, i2, g2, o2), (3, i3, g3, o3)):
        n = own_count(count)
        sources = near + far if count == 3 else near
        for t in range(TILES[count]):
            for row in range(2 * n):
                here = (t, pl.ds(row * N, N), slice(None))
                g[here] = plus(own[here], received(count, row, t, N, sources))
            rows = [g[t, pl.ds(z, 2 * n, stride=N), :] for z in range(N)]
            level = block_levels(rows, count)
            for k, v in enumerate(sent(level, count, 1)):
                put(up_ref, Z_UP[0], (count, 1, k, t), v)
            for k, v in enumerate(sent(level, count, -1)):
                put(down_ref, Z_DOWN[0], (count, -1, k, t), v)
            if count == 3:
                for k, v in enumerate(sent(level, count, 2)):
                    put(up2_ref, Z_UP2[0], (count, 2, k, t), v)
                for k, v in enumerate(sent(level, count, -2)):
                    put(down2_ref, Z_DOWN2[0], (count, -2, k, t), v)
            for b, band in enumerate(BANDS):
                for i in range(n):
                    o[t, b * n + i] = level.get(band, i)


def z_kernel(i1, i2, i3, up_in, down_in, up2_in, down2_in, one_ref, two_ref, three_ref, last_ref):
    near = [(1, Z_UP[0], up_in), (-1, Z_DOWN[0], down_in)]
    far = [(2, Z_UP2[0], up2_in), (-2, Z_DOWN2[0], down2_in)]
    for count, g, o in ((1, i1, one_ref), (2, i2, two_ref), (3, i3, three_ref)):
        n = own_count(count)
        sources = near + far if count == 3 else near
        for t in range(TILES[count]):
            hy, tile = divmod(t, TILES[count] // 2)
            lanes = pl.ds(128 * tile, 128)
            for row in range(2 * n):
                hz, z = divmod(row, n)
                value = plus(g[t, row], received(count, row, t, 2 * n, sources))
                for hx in range(2):
                    part = value[hx * n : hx * n + n]
                    band = hz * 4 + hy * 2 + hx
                    if band:
                        o[band - 1, z, :, lanes] = part
                    elif count == 3:
                        last_ref[z, :, lanes] = part


VMEM = pl.BlockSpec(memory_space=pltpu.VMEM)
PARAMS = pltpu.CompilerParams(vmem_limit_bytes=24 * 2**20)


def in_vmem(*shapes):
    return tuple(pltpu.VMEM(shape, F32) for shape in shapes)


def pinned(arrays):
    return [pltpu.with_memory_space_constraint(a, pltpu.VMEM) for a in arrays]


def call(kernel, arrays, out_shape, name, scratch=(), out_specs=None):
    arrays = pinned(arrays)
    return pl.pallas_call(
        kernel,
        out_shape=out_shape,
        in_specs=[VMEM] * len(arrays),
        out_specs=out_specs if out_specs is not None else tuple([VMEM] * len(out_shape)),
        scratch_shapes=scratch,
        compiler_params=PARAMS,
        name=name,
    )(*arrays)


def shift(x, axis, by):
    peers = lax.axis_size(axis)
    return lax.ppermute(x, axis, [(i, (i + by) % peers) for i in range(peers)])


def on_device(density):
    flat = density.reshape(N * N, 1024)
    to_down, to_up = pl.pallas_call(
        pack_kernel,
        grid=(1,),
        out_shape=in_vmem((64, 128), (64, 128)),
        in_specs=[pl.BlockSpec((256, 128), lambda i: (0, 0)), pl.BlockSpec((256, 128), lambda i: (0, 7))],
        out_specs=(VMEM, VMEM),
        compiler_params=PARAMS,
        name="pack_y",
    )(flat, flat)
    above = shift(to_down, "gy", -1)
    below = shift(to_up, "gy", 1)

    rows = {c: 2 * own_count(c) for c in ALL}
    outs = in_vmem(*[(TILES[c], rows[c] * N, 128) for c in ALL], *[(m[1], 128) for m in (X_UP, X_DOWN, X_FAR)])
    scratch = in_vmem((256, 640), (256, 640), (256, 128), (256, 128), *[(TILES[c], 256, 128) for c in ALL])
    a1, a2, a3, up, down, far = call(y_kernel, (flat, above, below), outs, "along_y", scratch)
    up = shift(up, "gx", 1)
    down = shift(down, "gx", -1)
    far = shift(far, "gx", 2)

    outs = in_vmem(
        *[(TILES[c], rows[c], rows[c], 128) for c in ALL], *[(m[1], 128) for m in (Z_UP, Z_DOWN, Z_UP2, Z_DOWN2)]
    )
    scratch = in_vmem(*[(TILES[c], rows[c] * N, 128) for c in ALL])
    b1, b2, b3, up, down, up2, down2 = call(x_kernel, (a1, a2, a3, up, down, far), outs, "along_x", scratch)
    up = shift(up, "gz", 1)
    down = shift(down, "gz", -1)
    up2 = shift(up2, "gz", 2)
    down2 = shift(down2, "gz", -2)

    outs = tuple(
        jax.ShapeDtypeStruct(s, F32) for s in ((7, 8, 8, 512), (7, 4, 4, 256), (7, 2, 2, 128), (2, 2, 128))
    )
    return call(z_kernel, (b1, b2, b3, up, down, up2, down2), outs, "along_z")


def solution(mesh):
    return jax.shard_map(
        on_device,
        mesh=mesh,
        in_specs=(P("gz", "gx", "gy"),),
        out_specs=(
            P(None, "gz", "gx", "gy"),
            P(None, "gz", "gx", "gy"),
            P(None, "gz", "gx", "gy"),
            P("gz", "gx", "gy"),
        ),
        check_vma=False,
    )
```

time: 151 us -> 59.8 us (0.40)
  starting transfers between devices: 73.4 us -> 40.5 us
  local copies, waits for them, and re-layouts: 31 us -> 1.22 us
  waiting for transfers between devices: 36.9 us -> 10.9 us
  other arithmetic: 7.61 us -> 0 us
  Pallas kernels: 0 us -> 5.99 us
    ppermute x18 -> x9, starting transfers between devices: 73.4 us -> 40.5 us  [shift(): return lax.ppermute(x, axis, [(i, (i + by) % peers) for i in range(peers)])]
    ppermute x18 -> x9, waiting for transfers between devices: 36.9 us -> 10.9 us  [shift(): return lax.ppermute(x, axis, [(i, (i + by) % peers) for i in range(peers)])]
    slice x14 -> x0, local copies, waits for them, and re-layouts: 17.3 us -> none  [the longest x7 16.3 us: lift_padded(): odds = lax.index_in_dim(paired, 1, dim + 1, False)]
    concatenate x7 -> x0, local copies, waits for them, and re-layouts: 7.3 us -> none  [the longest x6 6.99 us: padded_2(): x = jnp.concatenate([before, x, after], axis=dim)]
    pallas_call x0 -> x4, Pallas kernels: none -> 5.99 us  [the longest x3 5.87 us: call(): pl.pallas_call(kernel, out_shape=out_shape, in_specs=[VMEM] * len(arrays)...]
    unnamed x9 -> x2, local copies, waits for them, and re-layouts: 5.24 us -> 1.22 us
    concatenate x14 -> x0, other arithmetic: 3.01 us -> none  [the longest x6 2.4 us: lift_padded(): return jnp.concatenate([lower, upper], axis=0)]
    add x27 -> x0, other arithmetic: 2.71 us -> none  [the longest x9 0.96 us: lift_padded(): cut(evens, 1, half + 3, dim)]
  transfers between devices with their start and end apart: 18 -> 9, of which waited for: 13 -> 3; matrix products, arithmetic and copies ran while one was open for 1% -> 0% of each run, Pallas kernels for 0% -> 0%
where the time goes in v1:
time: 59.8 us; the launch traced here: 59.4 us
  starting transfers between devices  40.5 us (68%)
  waiting for transfers between devices  10.9 us (18%)
  Pallas kernels  5.99 us (10%)
  local copies, waits for them, and re-layouts  1.22 us (2%)
  between operations  0.75 us (1%)
    ppermute x9, starting transfers between devices, shift(): return lax.ppermute(x, axis, [(i, (i + by) % peers) for i in range(peers)])  40.5 us
    ppermute x9, waiting for transfers between devices, shift(): return lax.ppermute(x, axis, [(i, (i + by) % peers) for i in range(peers)])  10.9 us
    pallas_call x3, Pallas kernels, call(): pl.pallas_call(kernel, out_shape=out_shape, in_specs=[VMEM] * len(arrays)...  5.87 us
    unnamed x2, local copies, waits for them, and re-layouts  1.22 us
  transfers between devices with their start and end apart: 9, of which 3 were waited for; matrix products, arithmetic and copies ran while one was open for 0% of the time, Pallas kernels for 0%

profile of v1, /device:TPU:8, one launch (start us, length us, event | category | flops | bytes accessed | tf_op | source)
XLA Modules:
  0.0 59.4 jit_solution(7766276136572831736)
XLA Ops:
  0.6 0.0 copy-start
  0.6 1.2 %copy-done = f32[16,16,1024]{2,1,0:T(8,128)S(1)} copy-done((f32[16,16,1024]{2,1,0:T(8,128)S(1)}, f32[16,16,1024]{2,1,0:T(8,128)}, u32[]{:S(2)}) %copy-start) | copy-done | bytes 1048600
  1.9 0.1 pack_y.1
  2.0 5.3 %collective-permute-start = (f32[64,128]{1,0:T(8,128)S(1)}, f32[64,128]{1,0:T(8,128)S(1)}, u32[]{:S(2)}, u32[]{:S(2)}) collective-permute-start(f32[64,128]{1,0:T(8,128)S(1)} %get-tuple-element.19), channel_id=1, source_target_pairs={{0,96},{32,0},{64,32},{96,64},{1,97},{33,1},{65,33},{97,65},{2,98}... | collective-permute-start | bytes 98312 | tf_op jit(solution)/shard_map/ppermute | solution.py:336
  7.2 1.9 %collective-permute-start.1 = (f32[64,128]{1,0:T(8,128)S(1)}, f32[64,128]{1,0:T(8,128)S(1)}, u32[]{:S(2)}, u32[]{:S(2)}) collective-permute-start(f32[64,128]{1,0:T(8,128)S(1)} %get-tuple-element.20), channel_id=1, source_target_pairs={{0,32},{32,64},{64,96},{96,0},{1,33},{33,65},{65,97},{97,1},{2,34}... | collective-permute-start | bytes 98312 | tf_op jit(solution)/shard_map/ppermute | solution.py:336
  9.2 0.0 collective-permute-done.above_ref
  9.2 6.0 %collective-permute-done.1.below_ref = f32[64,128]{1,0:T(8,128)S(1)} collective-permute-done((f32[64,128]{1,0:T(8,128)S(1)}, f32[64,128]{1,0:T(8,128)S(1)}, u32[]{:S(2)}, u32[]{:S(2)}) %collective-permute-start.1) | collective-permute-done | bytes 32800 | tf_op jit(solution)/shard_map/ppermute | solution.py:336
  15.2 3.8 %along_y.1 = (f32[8,256,128]{2,1,0:T(8,128)S(1)}, f32[4,128,128]{2,1,0:T(8,128)S(1)}, f32[2,64,128]{2,1,0:T(8,128)S(1)}, f32[576,128]{1,0:T(8,128)S(1)}, f32[544,128]{1,0:T(8,128)S(1)}, /*index=5*/f32[96,128]{1,0:T(8,128)S(1)}) custom-call(f32[256,1024]{1,0:T(8,128)S(1)} %bitcast.3, f32[64,128]{1,0:T(8,128)S(1)} %collective-permute-done.above_ref, ...), custom_call_target="tpu_custom_call" | custom-call | tf_op jit(solution)/shard_map/along_y/pallas_call | solution.py:323
  19.0 1.9 %collective-permute-start.2 = (f32[576,128]{1,0:T(8,128)S(1)}, f32[576,128]{1,0:T(8,128)S(1)}, u32[]{:S(2)}, u32[]{:S(2)}) collective-permute-start(f32[576,128]{1,0:T(8,128)S(1)} %get-tuple-element.24), channel_id=1, source_target_pairs={{0,128},{128,256},{256,384},{384,0},{1,129},{129,257},{257,385},{3... | collective-permute-start | bytes 884744 | tf_op jit(solution)/shard_map/ppermute | solution.py:336
  20.9 3.6 %collective-permute-start.3 = (f32[544,128]{1,0:T(8,128)S(1)}, f32[544,128]{1,0:T(8,128)S(1)}, u32[]{:S(2)}, u32[]{:S(2)}) collective-permute-start(f32[544,128]{1,0:T(8,128)S(1)} %get-tuple-element.25), channel_id=1, source_target_pairs={{0,384},{128,0},{256,128},{384,256},{1,385},{129,1},{257,129},{385... | collective-permute-start | bytes 835592 | tf_op jit(solution)/shard_map/ppermute | solution.py:336
  24.5 4.4 %collective-permute-start.4 = (f32[96,128]{1,0:T(8,128)S(1)}, f32[96,128]{1,0:T(8,128)S(1)}, u32[]{:S(2)}, u32[]{:S(2)}) collective-permute-start(f32[96,128]{1,0:T(8,128)S(1)} %get-tuple-element.26), channel_id=1, source_target_pairs={{0,256},{128,384},{256,0},{384,128},{1,257},{129,385},{257,1},{385... | collective-permute-start | bytes 147464 | tf_op jit(solution)/shard_map/ppermute | solution.py:336
  28.9 3.6 %collective-permute-done.4.far_in = f32[96,128]{1,0:T(8,128)S(1)} collective-permute-done((f32[96,128]{1,0:T(8,128)S(1)}, f32[96,128]{1,0:T(8,128)S(1)}, u32[]{:S(2)}, u32[]{:S(2)}) %collective-permute-start.4) | collective-permute-done | bytes 49184 | tf_op jit(solution)/shard_map/ppermute | solution.py:336
  32.6 0.0 collective-permute-done.3.down_in
  32.6 0.0 collective-permute-done.2.up_in
  32.6 1.0 %along_x.1 = (f32[8,16,16,128]{3,2,1,0:T(8,128)S(1)}, f32[4,8,8,128]{3,2,1,0:T(8,128)S(1)}, f32[2,4,4,128]{3,2,1,0:T(4,128)S(1)}, f32[384,128]{1,0:T(8,128)S(1)}...) custom-call(f32[8,256,128]{2,1,0:T(8,128)S(1)} %get-tuple-element.21.i1, ...), custom_call_target="tpu_custom_call" | custom-call | tf_op jit(solution)/shard_map/along_x/pallas_call | solution.py:323
  33.6 2.3 %collective-permute-start.5 = (f32[384,128]{1,0:T(8,128)S(1)}, f32[384,128]{1,0:T(8,128)S(1)}, u32[]{:S(2)}, u32[]{:S(2)}) collective-permute-start(f32[384,128]{1,0:T(8,128)S(1)} %get-tuple-element.30), channel_id=1, source_target_pairs={{0,1},{1,2},{2,3},{3,4},{4,5},{5,6},{6,7},{7,8},{8,9},{9,10},{10,1... | collective-permute-start | bytes 589832 | tf_op jit(solution)/shard_map/ppermute | solution.py:336
  35.8 11.7 %collective-permute-start.6 = (f32[376,128]{1,0:T(8,128)S(1)}, f32[376,128]{1,0:T(8,128)S(1)}, u32[]{:S(2)}, u32[]{:S(2)}) collective-permute-start(f32[376,128]{1,0:T(8,128)S(1)} %get-tuple-element.31), channel_id=1, source_target_pairs={{0,31},{1,0},{2,1},{3,2},{4,3},{5,4},{6,5},{7,6},{8,7},{9,8},{10,9... | collective-permute-start | bytes 577544 | tf_op jit(solution)/shard_map/ppermute | solution.py:336
  47.5 1.9 %collective-permute-start.7 = (f32[16,128]{1,0:T(8,128)S(1)}, f32[16,128]{1,0:T(8,128)S(1)}, u32[]{:S(2)}, u32[]{:S(2)}) collective-permute-start(f32[16,128]{1,0:T(8,128)S(1)} %get-tuple-element.32), channel_id=1, source_target_pairs={{0,2},{1,3},{2,4},{3,5},{4,6},{5,7},{6,8},{7,9},{8,10},{9,11},{10,... | collective-permute-start | bytes 24584 | tf_op jit(solution)/shard_map/ppermute | solution.py:336
  49.4 7.5 %collective-permute-start.8 = (f32[8,128]{1,0:T(8,128)S(1)}, f32[8,128]{1,0:T(8,128)S(1)}, u32[]{:S(2)}, u32[]{:S(2)}) collective-permute-start(f32[8,128]{1,0:T(8,128)S(1)} %get-tuple-element.33), channel_id=1, source_target_pairs={{0,30},{1,31},{2,0},{3,1},{4,2},{5,3},{6,4},{7,5},{8,6},{9,7},{10,... | collective-permute-start | bytes 12296 | tf_op jit(solution)/shard_map/ppermute | solution.py:336
  57.0 1.3 %collective-permute-done.8.down2_in = f32[8,128]{1,0:T(8,128)S(1)} collective-permute-done((f32[8,128]{1,0:T(8,128)S(1)}, f32[8,128]{1,0:T(8,128)S(1)}, u32[]{:S(2)}, u32[]{:S(2)}) %collective-permute-start.8) | collective-permute-done | bytes 4128 | tf_op jit(solution)/shard_map/ppermute | solution.py:336
  58.3 0.0 collective-permute-done.7.up2_in
  58.3 0.0 collective-permute-done.6.down_in
  58.3 0.0 collective-permute-done.5.up_in
  58.3 1.1 %along_z.1 = (f32[7,8,8,512]{3,2,1,0:T(8,128)}, f32[7,4,4,256]{3,2,1,0:T(4,128)}, f32[7,2,2,128]{3,2,1,0:T(2,128)}, f32[2,2,128]{2,1,0:T(2,128)}) custom-call(f32[8,16,16,128]{3,2,1,0:T(8,128)S(1)} %get-tuple-element.27.i1, f32[4,8,8,128]{3,2,1,0:T(8,128)S(1)} %get-tuple-element.28.i2, f32[2,4,4,128]{3,2,1,0:T(4,128)S(1)} %get-tuple-element.29.i3, ...), custom_call_target="tpu_custom_call" | custom-call | tf_op jit(solution)/shard_map/along_z/pallas_call | solution.py:323
Async XLA Ops:
  0.6 1.2 %copy-start = (f32[16,16,1024]{2,1,0:T(8,128)S(1)}, f32[16,16,1024]{2,1,0:T(8,128)}, u32[]{:S(2)}) copy-start(f32[16,16,1024]{2,1,0:T(8,128)} %param.1) | copy-start | bytes 3145732
  2.0 7.2 %collective-permute-start = (f32[64,128]{1,0:T(8,128)S(1)}, f32[64,128]{1,0:T(8,128)S(1)}, u32[]{:S(2)}, u32[]{:S(2)}) collective-permute-start(f32[64,128]{1,0:T(8,128)S(1)} %get-tuple-element.19), channel_id=1, source_target_pairs={{0,96},{32,0},{64,32},{96,64},{1,97},{33,1},{65,33},{97,65},{2,98}... | collective-permute-start | bytes 98312 | tf_op jit(solution)/shard_map/ppermute | solution.py:336
  7.2 7.9 %collective-permute-start.1 = (f32[64,128]{1,0:T(8,128)S(1)}, f32[64,128]{1,0:T(8,128)S(1)}, u32[]{:S(2)}, u32[]{:S(2)}) collective-permute-start(f32[64,128]{1,0:T(8,128)S(1)} %get-tuple-element.20), channel_id=1, source_target_pairs={{0,32},{32,64},{64,96},{96,0},{1,33},{33,65},{65,97},{97,1},{2,34}... | collective-permute-start | bytes 98312 | tf_op jit(solution)/shard_map/ppermute | solution.py:336
  19.0 13.6 %collective-permute-start.2 = (f32[576,128]{1,0:T(8,128)S(1)}, f32[576,128]{1,0:T(8,128)S(1)}, u32[]{:S(2)}, u32[]{:S(2)}) collective-permute-start(f32[576,128]{1,0:T(8,128)S(1)} %get-tuple-element.24), channel_id=1, source_target_pairs={{0,128},{128,256},{256,384},{384,0},{1,129},{129,257},{257,385},{3... | collective-permute-start | bytes 884744 | tf_op jit(solution)/shard_map/ppermute | solution.py:336
  20.9 11.7 %collective-permute-start.3 = (f32[544,128]{1,0:T(8,128)S(1)}, f32[544,128]{1,0:T(8,128)S(1)}, u32[]{:S(2)}, u32[]{:S(2)}) collective-permute-start(f32[544,128]{1,0:T(8,128)S(1)} %get-tuple-element.25), channel_id=1, source_target_pairs={{0,384},{128,0},{256,128},{384,256},{1,385},{129,1},{257,129},{385... | collective-permute-start | bytes 835592 | tf_op jit(solution)/shard_map/ppermute | solution.py:336
  24.5 8.0 %collective-permute-start.4 = (f32[96,128]{1,0:T(8,128)S(1)}, f32[96,128]{1,0:T(8,128)S(1)}, u32[]{:S(2)}, u32[]{:S(2)}) collective-permute-start(f32[96,128]{1,0:T(8,128)S(1)} %get-tuple-element.26), channel_id=1, source_target_pairs={{0,256},{128,384},{256,0},{384,128},{1,257},{129,385},{257,1},{385... | collective-permute-start | bytes 147464 | tf_op jit(solution)/shard_map/ppermute | solution.py:336
  33.6 24.7 %collective-permute-start.5 = (f32[384,128]{1,0:T(8,128)S(1)}, f32[384,128]{1,0:T(8,128)S(1)}, u32[]{:S(2)}, u32[]{:S(2)}) collective-permute-start(f32[384,128]{1,0:T(8,128)S(1)} %get-tuple-element.30), channel_id=1, source_target_pairs={{0,1},{1,2},{2,3},{3,4},{4,5},{5,6},{6,7},{7,8},{8,9},{9,10},{10,1... | collective-permute-start | bytes 589832 | tf_op jit(solution)/shard_map/ppermute | solution.py:336
  35.8 22.5 %collective-permute-start.6 = (f32[376,128]{1,0:T(8,128)S(1)}, f32[376,128]{1,0:T(8,128)S(1)}, u32[]{:S(2)}, u32[]{:S(2)}) collective-permute-start(f32[376,128]{1,0:T(8,128)S(1)} %get-tuple-element.31), channel_id=1, source_target_pairs={{0,31},{1,0},{2,1},{3,2},{4,3},{5,4},{6,5},{7,6},{8,7},{9,8},{10,9... | collective-permute-start | bytes 577544 | tf_op jit(solution)/shard_map/ppermute | solution.py:336
  47.5 10.8 %collective-permute-start.7 = (f32[16,128]{1,0:T(8,128)S(1)}, f32[16,128]{1,0:T(8,128)S(1)}, u32[]{:S(2)}, u32[]{:S(2)}) collective-permute-start(f32[16,128]{1,0:T(8,128)S(1)} %get-tuple-element.32), channel_id=1, source_target_pairs={{0,2},{1,3},{2,4},{3,5},{4,6},{5,7},{6,8},{7,9},{8,10},{9,11},{10,... | collective-permute-start | bytes 24584 | tf_op jit(solution)/shard_map/ppermute | solution.py:336
  49.4 8.8 %collective-permute-start.8 = (f32[8,128]{1,0:T(8,128)S(1)}, f32[8,128]{1,0:T(8,128)S(1)}, u32[]{:S(2)}, u32[]{:S(2)}) collective-permute-start(f32[8,128]{1,0:T(8,128)S(1)} %get-tuple-element.33), channel_id=1, source_target_pairs={{0,30},{1,31},{2,0},{3,1},{4,2},{5,3},{6,4},{7,5},{8,6},{9,7},{10,... | collective-permute-start | bytes 12296 | tf_op jit(solution)/shard_map/ppermute | solution.py:336

commit v2 on v1

--- a/solution.py
+++ b/solution.py
@@ -181,14 +181,17 @@
     i = lax.broadcasted_iota(jnp.int32, (256, 256), 0)
     j = lax.broadcasted_iota(jnp.int32, (256, 256), 1)
     pick = (i == 2 * (j % 128) + j // 128).astype(jnp.bfloat16)
-    i = lax.broadcasted_iota(jnp.int32, (128, 256), 0)
-    j = lax.broadcasted_iota(jnp.int32, (128, 256), 1)
-    pick_halo = (i == (2 * (j % 128) + j // 128) % 128).astype(jnp.bfloat16)
     for t in range(half):
         both = split_dot(source(t), pick)
         even[:, pl.ds(128 * t, 128)] = both[:, :128]
         odd[:, pl.ds(128 * t, 128)] = both[:, 128:]
-    both = split_dot(halo(), pick_halo)
+    if halo is None:
+        both = jnp.zeros((256, 256), F32)
+    else:
+        i = lax.broadcasted_iota(jnp.int32, (128, 256), 0)
+        j = lax.broadcasted_iota(jnp.int32, (128, 256), 1)
+        pick_halo = (i == (2 * (j % 128) + j // 128) % 128).astype(jnp.bfloat16)
+        both = split_dot(halo[...], pick_halo)
     even[:, pl.ds(128 * half, 128)] = both[:, :128]
     odd[:, pl.ds(128 * half, 128)] = both[:, 128:]
     chunk = 16
@@ -212,37 +215,98 @@
     ref[pl.ds(places[key], value.shape[0]), :] = value
 
 
-def y_kernel(x_ref, above_ref, below_ref, o1, o2, o3, up_ref, down_ref, far_ref, even, odd, halo, halo2, g1, g2, g3):
+def x_lines(g, x):
+    return g[pl.ds(x, N, stride=N), :]
+
+
+def x_spill(level, count):
+    for message, offset in ((0, 1), (1, -1)) + (((2, 2), (2, -2)) if count == 3 else ()):
+        for k, v in enumerate(sent(level, count, offset)):
+            yield message, (count, offset, k), v
+
+
+X_PLACES = (X_UP[0], X_DOWN[0], X_FAR[0])
+
+
+def bulk_kernel(x_ref, g1, g2, g3, up_ref, down_ref, far_ref, even, odd, halo1, halo2):
+    def pair(g):
+        return lambda t: jnp.concatenate([g[2 * t], g[2 * t + 1]], axis=1)
+
+    y_level(lambda t: x_ref[:, pl.ds(256 * t, 256)], 8, None, even, odd, g1, halo1)
+    y_level(pair(g1), 4, halo1, even, odd, g2, halo2)
+    y_level(pair(g2), 2, halo2, even, odd, g3, None)
+    refs = (up_ref, down_ref, far_ref)
+    for count, g in ((1, g1), (2, g2), (3, g3)):
+        for t in range(TILES[count]):
+            level = block_levels([x_lines(g.at[t], x) for x in range(N)], count)
+            for m, key, v in x_spill(level, count):
+                put(refs[m], X_PLACES[m], key + (t,), v)
+
+
+def halo_matrix():
+    cells = np.eye(128)
+
+    def line(i):
+        if 1024 <= i < 1056:
+            return cells[i - 1024]
+        return cells[128 + i] if -32 <= i < 0 else None
+
+    columns = []
+    for count in ALL:
+        level = Level(line)
+        line = functools.partial(level.get, "low")
+        n = 1024 >> count
+        for band, start in (("low", 0), ("high", n - 32), ("high", 0), ("low", n - 32)):
+            values = [level.get(band, start + i) for i in range(32)]
+            columns += [np.zeros(128) if v is None else v for v in values]
+    return np.stack(columns, axis=1).astype(np.float32)
+
+
+def edges(count, t, low, high):
+    half = TILES[count] // 2
+    value, t = (low, t) if t < half else (high, t - half)
+    if t not in (0, half - 1):
+        return None
+    lane = lax.broadcasted_iota(jnp.int32, value.shape, 1)
+    keep = lane < 0
+    if t == 0:
+        keep |= lane < 32
+    if t == half - 1:
+        keep |= lane >= 96
+    return jnp.where(keep, value, 0.0)
+
+
+def halo_kernel(above_ref, below_ref, w_ref, up_in, down_in, far_in, d_ref, up_ref, down_ref, far_ref, halo):
     lane = lax.broadcasted_iota(jnp.int32, (64, 128), 1)
     for g in range(4):
         a, b = above_ref[...], below_ref[...]
         a = pltpu.roll(a, 128 - 32 * g, 1) if g else a
         b = pltpu.roll(b, 96 - 32 * g, 1) if g < 3 else b
         halo[pl.ds(64 * g, 64), :] = jnp.where(lane < 32, a, jnp.where(lane >= 96, b, 0.0))
-
-    def pair(g):
-        return lambda t: jnp.concatenate([g[2 * t], g[2 * t + 1]], axis=1)
-
-    y_level(lambda t: x_ref[:, pl.ds(256 * t, 256)], 8, lambda: halo[...], even, odd, g1, halo2)
-    y_level(pair(g1), 4, lambda: halo2[...], even, odd, g2, halo)
-    y_level(pair(g2), 2, lambda: halo[...], even, odd, g3, None)
-
+    both = jnp.dot(halo[...], w_ref[...], precision=lax.Precision.HIGHEST, preferred_element_type=F32)
+    for c in range(3):
+        d_ref[c] = both[:, 128 * c : 128 * c + 128]
+    ins, refs = (up_in, down_in, far_in), (up_ref, down_ref, far_ref)
+    for count in ALL:
+        level = block_levels([x_lines(d_ref.at[count - 1], x) for x in range(N)], count)
+        for m, key, v in x_spill(level, count):
+            turned = pltpu.roll(v, 64, 1)
+            for t in range(TILES[count]):
+                own = ins[m][pl.ds(X_PLACES[m][key + (t,)], N), :]
+                put(refs[m], X_PLACES[m], key + (t,), plus(own, edges(count, t, v, turned)))
+
+
+def own_x_kernel(g1, g2, g3, d_ref, o1, o2, o3):
     for count, g, o in ((1, g1, o1), (2, g2, o2), (3, g3, o3)):
         n = own_count(count)
-        for t in range(TILES[count]):
-            rows = [g[t, pl.ds(x, N, stride=N), :] for x in range(N)]
-            level = block_levels(rows, count)
-            for k, v in enumerate(sent(level, count, 1)):
-                put(up_ref, X_UP[0], (count, 1, k, t), v)
-            for k, v in enumerate(sent(level, count, -1)):
-                put(down_ref, X_DOWN[0], (count, -1, k, t), v)
-            if count == 3:
-                for offset in (2, -2):
-                    for k, v in enumerate(sent(level, count, offset)):
-                        put(far_ref, X_FAR[0], (count, offset, k, t), v)
-            for b, band in enumerate(BANDS):
-                for i in range(n):
-                    o[t, pl.ds((b * n + i) * N, N), :] = level.get(band, i)
+        halo = block_levels([x_lines(d_ref.at[count - 1], x) for x in range(N)], count)
+        blocks = [block_levels([x_lines(g.at[t], x) for x in range(N)], count) for t in range(TILES[count])]
+        for b, band in enumerate(BANDS):
+            for i in range(n):
+                v = halo.get(band, i)
+                turned = pltpu.roll(v, 64, 1)
+                for t in range(TILES[count]):
+                    o[t, pl.ds((b * n + i) * N, N), :] = plus(blocks[t].get(band, i), edges(count, t, v, turned))
 
 
 def received(count, row, t, height, sources):
@@ -259,18 +323,21 @@
     return total
 
 
-def x_kernel(i1, i2, i3, up_in, down_in, far_in, o1, o2, o3, up_ref, down_ref, up2_ref, down2_ref, g1, g2, g3):
+def z_lines(g, t, count):
+    return [g[t, pl.ds(z, 2 * own_count(count), stride=N), :] for z in range(N)]
+
+
+def x_kernel(i1, i2, i3, up_in, down_in, far_in, o1, o2, o3, up_ref, down_ref, up2_ref, down2_ref):
     near = [(1, X_UP[0], up_in), (-1, X_DOWN[0], down_in)]
     far = [(2, X_FAR[0], far_in), (-2, X_FAR[0], far_in)]
-    for count, own, g, o in ((1, i1, g1, o1), (2, i2, g2, o2), (3, i3, g3, o3)):
+    for count, own, g in ((1, i1, o1), (2, i2, o2), (3, i3, o3)):
         n = own_count(count)
         sources = near + far if count == 3 else near
         for t in range(TILES[count]):
             for row in range(2 * n):
                 here = (t, pl.ds(row * N, N), slice(None))
                 g[here] = plus(own[here], received(count, row, t, N, sources))
-            rows = [g[t, pl.ds(z, 2 * n, stride=N), :] for z in range(N)]
-            level = block_levels(rows, count)
+            level = block_levels(z_lines(g, t, count), count)
             for k, v in enumerate(sent(level, count, 1)):
                 put(up_ref, Z_UP[0], (count, 1, k, t), v)
             for k, v in enumerate(sent(level, count, -1)):
@@ -280,6 +347,13 @@
                     put(up2_ref, Z_UP2[0], (count, 2, k, t), v)
                 for k, v in enumerate(sent(level, count, -2)):
                     put(down2_ref, Z_DOWN2[0], (count, -2, k, t), v)
+
+
+def own_z_kernel(g1, g2, g3, o1, o2, o3):
+    for count, g, o in ((1, g1, o1), (2, g2, o2), (3, g3, o3)):
+        n = own_count(count)
+        for t in range(TILES[count]):
+            level = block_levels(z_lines(g, t, count), count)
             for b, band in enumerate(BANDS):
                 for i in range(n):
                     o[t, b * n + i] = level.get(band, i)
@@ -314,19 +388,20 @@
     return tuple(pltpu.VMEM(shape, F32) for shape in shapes)
 
 
-def pinned(arrays):
-    return [pltpu.with_memory_space_constraint(a, pltpu.VMEM) for a in arrays]
-
-
-def call(kernel, arrays, out_shape, name, scratch=(), out_specs=None):
+def pinned(arrays, space=pltpu.VMEM):
+    return [pltpu.with_memory_space_constraint(a, space) for a in arrays]
+
+
+def call(kernel, arrays, out_shape, name, scratch=(), moved=4):
     arrays = pinned(arrays)
     return pl.pallas_call(
         kernel,
         out_shape=out_shape,
         in_specs=[VMEM] * len(arrays),
-        out_specs=out_specs if out_specs is not None else tuple([VMEM] * len(out_shape)),
+        out_specs=tuple([VMEM] * len(out_shape)),
         scratch_shapes=scratch,
         compiler_params=PARAMS,
+        cost_estimate=pl.CostEstimate(flops=0, transcendentals=0, bytes_accessed=moved * 2**20),
         name=name,
     )(*arrays)
 
@@ -338,6 +413,7 @@
 
 def on_device(density):
     flat = density.reshape(N * N, 1024)
+    in_hbm = pinned([flat], pltpu.HBM)[0]
     to_down, to_up = pl.pallas_call(
         pack_kernel,
         grid=(1,),
@@ -346,32 +422,39 @@
         out_specs=(VMEM, VMEM),
         compiler_params=PARAMS,
         name="pack_y",
-    )(flat, flat)
+    )(in_hbm, in_hbm)
     above = shift(to_down, "gy", -1)
     below = shift(to_up, "gy", 1)
 
     rows = {c: 2 * own_count(c) for c in ALL}
-    outs = in_vmem(*[(TILES[c], rows[c] * N, 128) for c in ALL], *[(m[1], 128) for m in (X_UP, X_DOWN, X_FAR)])
-    scratch = in_vmem((256, 640), (256, 640), (256, 128), (256, 128), *[(TILES[c], 256, 128) for c in ALL])
-    a1, a2, a3, up, down, far = call(y_kernel, (flat, above, below), outs, "along_y", scratch)
+    messages = in_vmem(*[(m[1], 128) for m in (X_UP, X_DOWN, X_FAR)])
+    outs = in_vmem(*[(TILES[c], 256, 128) for c in ALL]) + messages
+    scratch = in_vmem((256, 640), (256, 640), (256, 128), (256, 128))
+    g1, g2, g3, up, down, far = call(bulk_kernel, (flat,), outs, "own_y", scratch, 12)
+    outs = in_vmem((3, 256, 128)) + messages
+    weights = jnp.asarray(halo_matrix())
+    d, up, down, far = call(
+        halo_kernel, (above, below, weights, up, down, far), outs, "halo_y", in_vmem((256, 128))
+    )
     up = shift(up, "gx", 1)
     down = shift(down, "gx", -1)
     far = shift(far, "gx", 2)
 
-    outs = in_vmem(
-        *[(TILES[c], rows[c], rows[c], 128) for c in ALL], *[(m[1], 128) for m in (Z_UP, Z_DOWN, Z_UP2, Z_DOWN2)]
-    )
-    scratch = in_vmem(*[(TILES[c], rows[c] * N, 128) for c in ALL])
-    b1, b2, b3, up, down, up2, down2 = call(x_kernel, (a1, a2, a3, up, down, far), outs, "along_x", scratch)
+    blocks = in_vmem(*[(TILES[c], rows[c] * N, 128) for c in ALL])
+    own = call(own_x_kernel, (g1, g2, g3, d), blocks, "own_x", (), 8)
+    outs = blocks + in_vmem(*[(m[1], 128) for m in (Z_UP, Z_DOWN, Z_UP2, Z_DOWN2)])
+    a1, a2, a3, up, down, up2, down2 = call(x_kernel, (*own, up, down, far), outs, "spill_x")
     up = shift(up, "gz", 1)
     down = shift(down, "gz", -1)
     up2 = shift(up2, "gz", 2)
     down2 = shift(down2, "gz", -2)
 
+    outs = in_vmem(*[(TILES[c], rows[c], rows[c], 128) for c in ALL])
+    own = call(own_z_kernel, (a1, a2, a3), outs, "own_z", (), 8)
     outs = tuple(
         jax.ShapeDtypeStruct(s, F32) for s in ((7, 8, 8, 512), (7, 4, 4, 256), (7, 2, 2, 128), (2, 2, 128))
     )
-    return call(z_kernel, (b1, b2, b3, up, down, up2, down2), outs, "along_z")
+    return call(z_kernel, (*own, up, down, up2, down2), outs, "spill_z")
 
 
 def solution(mesh):

time: 59.8 us -> 56.4 us (0.943)
  waiting for transfers between devices: 10.9 us -> 5.35 us
  Pallas kernels: 5.99 us -> 9.23 us
  local copies, waits for them, and re-layouts: 1.22 us -> 0.01 us
    ppermute x9, waiting for transfers between devices: 10.9 us -> 5.35 us  [shift(): return lax.ppermute(x, axis, [(i, (i + by) % peers) for i in range(peers)])]
    pallas_call x3 -> x6, Pallas kernels: 5.87 us -> 8.06 us  [call(): pl.pallas_call(kernel, out_shape=out_shape, in_specs=[VMEM] * len(arrays)...]
    unnamed x2 -> x4, local copies, waits for them, and re-layouts: 1.22 us -> 0.01 us
    pallas_call x1, Pallas kernels: 0.11 us -> 1.17 us  [on_device(): pl.pallas_call(pack_kernel, grid=(1,), out_shape=in_vmem((64, 128), (64,...]
  transfers between devices with their start and end apart: 9 -> 9, of which waited for: 3 -> 3; matrix products, arithmetic and copies ran while one was open for 0% -> 0% of each run, Pallas kernels for 0% -> 10%
where the time goes in v2:
time: 56.4 us; the launch traced here: 56 us
  starting transfers between devices  40.7 us (72%)
  Pallas kernels  9.23 us (16%)
  waiting for transfers between devices  5.35 us (9%)
  between operations  0.78 us (1%)
    ppermute x9, starting transfers between devices, shift(): return lax.ppermute(x, axis, [(i, (i + by) % peers) for i in range(peers)])  40.7 us
    pallas_call x6, Pallas kernels, call(): pl.pallas_call(kernel, out_shape=out_shape, in_specs=[VMEM] * len(arrays)...  8.06 us
    ppermute x9, waiting for transfers between devices, shift(): return lax.ppermute(x, axis, [(i, (i + by) % peers) for i in range(peers)])  5.35 us
    pallas_call x1, Pallas kernels, on_device(): pl.pallas_call(pack_kernel, grid=(1,), out_shape=in_vmem((64, 128), (64,...  1.17 us
  transfers between devices with their start and end apart: 9, of which 3 were waited for; matrix products, arithmetic and copies ran while one was open for 0% of the time, Pallas kernels for 10%

profile of v2, /device:TPU:8, one launch (start us, length us, event | category | flops | bytes accessed | tf_op | source)
XLA Modules:
  0.0 56.0 jit_solution(15075582335078437093)
XLA Ops:
  0.6 0.0 copy-start
  0.6 1.2 %pack_y.1 = (f32[64,128]{1,0:T(8,128)S(1)}, f32[64,128]{1,0:T(8,128)S(1)}) custom-call(f32[256,1024]{1,0:T(8,128)} %bitcast.1, f32[256,1024]{1,0:T(8,128)} %bitcast.2), custom_call_target="tpu_custom_call" | custom-call | tf_op jit(solution)/shard_map/pack_y/pallas_call | solution.py:417
  1.8 5.3 %collective-permute-start = (f32[64,128]{1,0:T(8,128)S(1)}, f32[64,128]{1,0:T(8,128)S(1)}, u32[]{:S(2)}, u32[]{:S(2)}) collective-permute-start(f32[64,128]{1,0:T(8,128)S(1)} %get-tuple-element.32), channel_id=1, source_target_pairs={{0,96},{32,0},{64,32},{96,64},{1,97},{33,1},{65,33},{97,65},{2,98}... | collective-permute-start | bytes 98312 | tf_op jit(solution)/shard_map/ppermute | solution.py:411
  7.1 0.0 copy-start.1
  7.1 2.1 %collective-permute-start.1 = (f32[64,128]{1,0:T(8,128)S(1)}, f32[64,128]{1,0:T(8,128)S(1)}, u32[]{:S(2)}, u32[]{:S(2)}) collective-permute-start(f32[64,128]{1,0:T(8,128)S(1)} %get-tuple-element.33), channel_id=1, source_target_pairs={{0,32},{32,64},{64,96},{96,0},{1,33},{33,65},{65,97},{97,1},{2,34}... | collective-permute-start | bytes 98312 | tf_op jit(solution)/shard_map/ppermute | solution.py:411
  9.2 0.0 copy-done
  9.2 3.3 %own_y.1 = (f32[8,256,128]{2,1,0:T(8,128)S(1)}, f32[4,256,128]{2,1,0:T(8,128)S(1)}, f32[2,256,128]{2,1,0:T(8,128)S(1)}, f32[576,128]{1,0:T(8,128)S(1)}, f32[544,128]{1,0:T(8,128)S(1)}, /*index=5*/f32[96,128]{1,0:T(8,128)S(1)}) custom-call(f32[256,1024]{1,0:T(8,128)S(1)} %bitcast.3), custom_call_target="tpu_custom_call" | custom-call | bytes 12582912 | tf_op jit(solution)/shard_map/own_y/pallas_call | solution.py:397
  12.4 0.0 collective-permute-done.above_ref
  12.4 2.7 %collective-permute-done.1.below_ref = f32[64,128]{1,0:T(8,128)S(1)} collective-permute-done((f32[64,128]{1,0:T(8,128)S(1)}, f32[64,128]{1,0:T(8,128)S(1)}, u32[]{:S(2)}, u32[]{:S(2)}) %collective-permute-start.1) | collective-permute-done | bytes 32800 | tf_op jit(solution)/shard_map/ppermute | solution.py:411
  15.2 0.0 copy-done.1
  15.2 0.8 %halo_y.1 = (f32[3,256,128]{2,1,0:T(8,128)S(1)}, f32[576,128]{1,0:T(8,128)S(1)}, f32[544,128]{1,0:T(8,128)S(1)}, f32[96,128]{1,0:T(8,128)S(1)}) custom-call(f32[64,128]{1,0:T(8,128)S(1)} %collective-permute-done.above_ref, f32[64,128]{1,0:T(8,128)S(1)} %collective-permute-done.1.below_ref, f32[128,384]{1,0:T(8,128)S(1)} %copy-done.1, ...), custom_call_target="tpu_custom_call" | custom-call | bytes 4194304 | tf_op jit(solution)/shard_map/halo_y/pallas_call | solution.py:397
  16.0 1.9 %collective-permute-start.2 = (f32[576,128]{1,0:T(8,128)S(1)}, f32[576,128]{1,0:T(8,128)S(1)}, u32[]{:S(2)}, u32[]{:S(2)}) collective-permute-start(f32[576,128]{1,0:T(8,128)S(1)} %get-tuple-element.41), channel_id=1, source_target_pairs={{0,128},{128,256},{256,384},{384,0},{1,129},{129,257},{257,385},{3... | collective-permute-start | bytes 884744 | tf_op jit(solution)/shard_map/ppermute | solution.py:411
  17.9 3.6 %collective-permute-start.3 = (f32[544,128]{1,0:T(8,128)S(1)}, f32[544,128]{1,0:T(8,128)S(1)}, u32[]{:S(2)}, u32[]{:S(2)}) collective-permute-start(f32[544,128]{1,0:T(8,128)S(1)} %get-tuple-element.42), channel_id=1, source_target_pairs={{0,384},{128,0},{256,128},{384,256},{1,385},{129,1},{257,129},{385... | collective-permute-start | bytes 835592 | tf_op jit(solution)/shard_map/ppermute | solution.py:411
  21.6 4.6 %collective-permute-start.4 = (f32[96,128]{1,0:T(8,128)S(1)}, f32[96,128]{1,0:T(8,128)S(1)}, u32[]{:S(2)}, u32[]{:S(2)}) collective-permute-start(f32[96,128]{1,0:T(8,128)S(1)} %get-tuple-element.43), channel_id=1, source_target_pairs={{0,256},{128,384},{256,0},{384,128},{1,257},{129,385},{257,1},{385... | collective-permute-start | bytes 147464 | tf_op jit(solution)/shard_map/ppermute | solution.py:411
  26.2 1.6 %own_x.1 = (f32[8,256,128]{2,1,0:T(8,128)S(1)}, f32[4,128,128]{2,1,0:T(8,128)S(1)}, f32[2,64,128]{2,1,0:T(8,128)S(1)}) custom-call(f32[8,256,128]{2,1,0:T(8,128)S(1)} %get-tuple-element.29.g1, f32[4,256,128]{2,1,0:T(8,128)S(1)} %get-tuple-element.30.g2, f32[2,256,128]{2,1,0:T(8,128)S(1)} %get-tuple-element.31.g3, f32[3,256,128]{2,1,0:T(8,128)S(1)} %get-tuple-element.37.d_ref), custom_call_target="tpu_custom_call" | custom-call | bytes 8388608 | tf_op jit(solution)/shard_map/own_x/pallas_call | solution.py:397
  27.8 2.1 %collective-permute-done.4.far_in = f32[96,128]{1,0:T(8,128)S(1)} collective-permute-done((f32[96,128]{1,0:T(8,128)S(1)}, f32[96,128]{1,0:T(8,128)S(1)}, u32[]{:S(2)}, u32[]{:S(2)}) %collective-permute-start.4) | collective-permute-done | bytes 49184 | tf_op jit(solution)/shard_map/ppermute | solution.py:411
  29.8 0.0 collective-permute-done.3.down_in
  29.8 0.0 collective-permute-done.2.up_in
  29.8 0.6 %spill_x.1 = (f32[8,256,128]{2,1,0:T(8,128)S(1)}, f32[4,128,128]{2,1,0:T(8,128)S(1)}, f32[2,64,128]{2,1,0:T(8,128)S(1)}, f32[384,128]{1,0:T(8,128)S(1)}, f32[376...) custom-call(f32[8,256,128]{2,1,0:T(8,128)S(1)} %get-tuple-element.38.i1, ...), custom_call_target="tpu_custom_call" | custom-call | bytes 4194304 | tf_op jit(solution)/shard_map/spill_x/pallas_call | solution.py:397
  30.4 2.0 %collective-permute-start.5 = (f32[384,128]{1,0:T(8,128)S(1)}, f32[384,128]{1,0:T(8,128)S(1)}, u32[]{:S(2)}, u32[]{:S(2)}) collective-permute-start(f32[384,128]{1,0:T(8,128)S(1)} %get-tuple-element.50), channel_id=1, source_target_pairs={{0,1},{1,2},{2,3},{3,4},{4,5},{5,6},{6,7},{7,8},{8,9},{9,10},{10,1... | collective-permute-start | bytes 589832 | tf_op jit(solution)/shard_map/ppermute | solution.py:411
  32.5 11.7 %collective-permute-start.6 = (f32[376,128]{1,0:T(8,128)S(1)}, f32[376,128]{1,0:T(8,128)S(1)}, u32[]{:S(2)}, u32[]{:S(2)}) collective-permute-start(f32[376,128]{1,0:T(8,128)S(1)} %get-tuple-element.51), channel_id=1, source_target_pairs={{0,31},{1,0},{2,1},{3,2},{4,3},{5,4},{6,5},{7,6},{8,7},{9,8},{10,9... | collective-permute-start | bytes 577544 | tf_op jit(solution)/shard_map/ppermute | solution.py:411
  44.1 1.9 %collective-permute-start.7 = (f32[16,128]{1,0:T(8,128)S(1)}, f32[16,128]{1,0:T(8,128)S(1)}, u32[]{:S(2)}, u32[]{:S(2)}) collective-permute-start(f32[16,128]{1,0:T(8,128)S(1)} %get-tuple-element.52), channel_id=1, source_target_pairs={{0,2},{1,3},{2,4},{3,5},{4,6},{5,7},{6,8},{7,9},{8,10},{9,11},{10,... | collective-permute-start | bytes 24584 | tf_op jit(solution)/shard_map/ppermute | solution.py:411
  46.1 7.5 %collective-permute-start.8 = (f32[8,128]{1,0:T(8,128)S(1)}, f32[8,128]{1,0:T(8,128)S(1)}, u32[]{:S(2)}, u32[]{:S(2)}) collective-permute-start(f32[8,128]{1,0:T(8,128)S(1)} %get-tuple-element.53), channel_id=1, source_target_pairs={{0,30},{1,31},{2,0},{3,1},{4,2},{5,3},{6,4},{7,5},{8,6},{9,7},{10,... | collective-permute-start | bytes 12296 | tf_op jit(solution)/shard_map/ppermute | solution.py:411
  53.6 0.7 %own_z.1 = (f32[8,16,16,128]{3,2,1,0:T(8,128)S(1)}, f32[4,8,8,128]{3,2,1,0:T(8,128)S(1)}, f32[2,4,4,128]{3,2,1,0:T(4,128)S(1)}) custom-call(f32[8,256,128]{2,1,0:T(8,128)S(1)} %get-tuple-element.44.g1, f32[4,128,128]{2,1,0:T(8,128)S(1)} %get-tuple-element.45.g2, f32[2,64,128]{2,1,0:T(8,128)S(1)} %get-tuple-element.46.g3), custom_call_target="tpu_custom_call" | custom-call | bytes 8388608 | tf_op jit(solution)/shard_map/own_z/pallas_call | solution.py:397
  54.3 0.6 %collective-permute-done.8.down2_in = f32[8,128]{1,0:T(8,128)S(1)} collective-permute-done((f32[8,128]{1,0:T(8,128)S(1)}, f32[8,128]{1,0:T(8,128)S(1)}, u32[]{:S(2)}, u32[]{:S(2)}) %collective-permute-start.8) | collective-permute-done | bytes 4128 | tf_op jit(solution)/shard_map/ppermute | solution.py:411
  54.9 0.0 collective-permute-done.7.up2_in
  54.9 0.0 collective-permute-done.6.down_in
  54.9 0.0 collective-permute-done.5.up_in
  54.9 1.1 %spill_z.1 = (f32[7,8,8,512]{3,2,1,0:T(8,128)}, f32[7,4,4,256]{3,2,1,0:T(4,128)}, f32[7,2,2,128]{3,2,1,0:T(2,128)}, f32[2,2,128]{2,1,0:T(2,128)}) custom-call(f32[8,16,16,128]{3,2,1,0:T(8,128)S(1)} %get-tuple-element.47.i1, f32[4,8,8,128]{3,2,1,0:T(8,128)S(1)} %get-tuple-element.48.i2, f32[2,4,4,128]{3,2,1,0:T(4,128)S(1)} %get-tuple-element.49.i3, ...), custom_call_target="tpu_custom_call" | custom-call | bytes 4194304 | tf_op jit(solution)/shard_map/spill_z/pallas_call | solution.py:397
Async XLA Ops:
  0.6 8.5 %copy-start = (f32[16,16,1024]{2,1,0:T(8,128)S(1)}, f32[16,16,1024]{2,1,0:T(8,128)}, u32[]{:S(2)}) copy-start(f32[16,16,1024]{2,1,0:T(8,128)} %param.2) | copy-start | bytes 3145732
  1.8 10.6 %collective-permute-start = (f32[64,128]{1,0:T(8,128)S(1)}, f32[64,128]{1,0:T(8,128)S(1)}, u32[]{:S(2)}, u32[]{:S(2)}) collective-permute-start(f32[64,128]{1,0:T(8,128)S(1)} %get-tuple-element.32), channel_id=1, source_target_pairs={{0,96},{32,0},{64,32},{96,64},{1,97},{33,1},{65,33},{97,65},{2,98}... | collective-permute-start | bytes 98312 | tf_op jit(solution)/shard_map/ppermute | solution.py:411
  7.1 8.1 %copy-start.1 = (f32[128,384]{1,0:T(8,128)S(1)}, f32[128,384]{1,0:T(8,128)}, u32[]{:S(2)}) copy-start(f32[128,384]{1,0:T(8,128)} %constant.2.clone.w_ref) | copy-start | bytes 589828
  7.1 8.0 %collective-permute-start.1 = (f32[64,128]{1,0:T(8,128)S(1)}, f32[64,128]{1,0:T(8,128)S(1)}, u32[]{:S(2)}, u32[]{:S(2)}) collective-permute-start(f32[64,128]{1,0:T(8,128)S(1)} %get-tuple-element.33), channel_id=1, source_target_pairs={{0,32},{32,64},{64,96},{96,0},{1,33},{33,65},{65,97},{97,1},{2,34}... | collective-permute-start | bytes 98312 | tf_op jit(solution)/shard_map/ppermute | solution.py:411
  16.0 13.8 %collective-permute-start.2 = (f32[576,128]{1,0:T(8,128)S(1)}, f32[576,128]{1,0:T(8,128)S(1)}, u32[]{:S(2)}, u32[]{:S(2)}) collective-permute-start(f32[576,128]{1,0:T(8,128)S(1)} %get-tuple-element.41), channel_id=1, source_target_pairs={{0,128},{128,256},{256,384},{384,0},{1,129},{129,257},{257,385},{3... | collective-permute-start | bytes 884744 | tf_op jit(solution)/shard_map/ppermute | solution.py:411
  17.9 11.9 %collective-permute-start.3 = (f32[544,128]{1,0:T(8,128)S(1)}, f32[544,128]{1,0:T(8,128)S(1)}, u32[]{:S(2)}, u32[]{:S(2)}) collective-permute-start(f32[544,128]{1,0:T(8,128)S(1)} %get-tuple-element.42), channel_id=1, source_target_pairs={{0,384},{128,0},{256,128},{384,256},{1,385},{129,1},{257,129},{385... | collective-permute-start | bytes 835592 | tf_op jit(solution)/shard_map/ppermute | solution.py:411
  21.6 8.3 %collective-permute-start.4 = (f32[96,128]{1,0:T(8,128)S(1)}, f32[96,128]{1,0:T(8,128)S(1)}, u32[]{:S(2)}, u32[]{:S(2)}) collective-permute-start(f32[96,128]{1,0:T(8,128)S(1)} %get-tuple-element.43), channel_id=1, source_target_pairs={{0,256},{128,384},{256,0},{384,128},{1,257},{129,385},{257,1},{385... | collective-permute-start | bytes 147464 | tf_op jit(solution)/shard_map/ppermute | solution.py:411
  30.4 24.5 %collective-permute-start.5 = (f32[384,128]{1,0:T(8,128)S(1)}, f32[384,128]{1,0:T(8,128)S(1)}, u32[]{:S(2)}, u32[]{:S(2)}) collective-permute-start(f32[384,128]{1,0:T(8,128)S(1)} %get-tuple-element.50), channel_id=1, source_target_pairs={{0,1},{1,2},{2,3},{3,4},{4,5},{5,6},{6,7},{7,8},{8,9},{9,10},{10,1... | collective-permute-start | bytes 589832 | tf_op jit(solution)/shard_map/ppermute | solution.py:411
  32.5 22.5 %collective-permute-start.6 = (f32[376,128]{1,0:T(8,128)S(1)}, f32[376,128]{1,0:T(8,128)S(1)}, u32[]{:S(2)}, u32[]{:S(2)}) collective-permute-start(f32[376,128]{1,0:T(8,128)S(1)} %get-tuple-element.51), channel_id=1, source_target_pairs={{0,31},{1,0},{2,1},{3,2},{4,3},{5,4},{6,5},{7,6},{8,7},{9,8},{10,9... | collective-permute-start | bytes 577544 | tf_op jit(solution)/shard_map/ppermute | solution.py:411
  44.1 10.8 %collective-permute-start.7 = (f32[16,128]{1,0:T(8,128)S(1)}, f32[16,128]{1,0:T(8,128)S(1)}, u32[]{:S(2)}, u32[]{:S(2)}) collective-permute-start(f32[16,128]{1,0:T(8,128)S(1)} %get-tuple-element.52), channel_id=1, source_target_pairs={{0,2},{1,3},{2,4},{3,5},{4,6},{5,7},{6,8},{7,9},{8,10},{9,11},{10,... | collective-permute-start | bytes 24584 | tf_op jit(solution)/shard_map/ppermute | solution.py:411
  46.1 8.8 %collective-permute-start.8 = (f32[8,128]{1,0:T(8,128)S(1)}, f32[8,128]{1,0:T(8,128)S(1)}, u32[]{:S(2)}, u32[]{:S(2)}) collective-permute-start(f32[8,128]{1,0:T(8,128)S(1)} %get-tuple-element.53), channel_id=1, source_target_pairs={{0,30},{1,31},{2,0},{3,1},{4,2},{5,3},{6,4},{7,5},{8,6},{9,7},{10,... | collective-permute-start | bytes 12296 | tf_op jit(solution)/shard_map/ppermute | solution.py:411

commit v3 on v2

--- a/solution.py
+++ b/solution.py
@@ -142,8 +142,7 @@
 X_HEIGHT = {1: N, 2: N, 3: N}
 Z_HEIGHT = {1: 16, 2: 8, 3: 4}
 ALL = (1, 2, 3)
-X_UP = message_places(X_HEIGHT, (1,), ALL)
-X_DOWN = message_places(X_HEIGHT, (-1,), ALL)
+X_NEAR = message_places(X_HEIGHT, (1,), ALL)
 X_FAR = message_places(X_HEIGHT, (2, -2), (3,))
 Z_UP = message_places(Z_HEIGHT, (1,), ALL)
 Z_DOWN = message_places(Z_HEIGHT, (-1,), ALL)
@@ -219,28 +218,34 @@
     return g[pl.ds(x, N, stride=N), :]
 
 
-def x_spill(level, count):
-    for message, offset in ((0, 1), (1, -1)) + (((2, 2), (2, -2)) if count == 3 else ()):
+def x_near(level, count, even):
+    up, down = sent(level, count, 1), sent(level, count, -1)
+    for k, v in enumerate(up):
+        w = down[k] if k < len(down) else v
+        yield (count, 1, k), jnp.where(even, v, w), jnp.where(even, w, v)
+
+
+def x_far(level, count):
+    for offset in (2, -2):
         for k, v in enumerate(sent(level, count, offset)):
-            yield message, (count, offset, k), v
-
-
-X_PLACES = (X_UP[0], X_DOWN[0], X_FAR[0])
-
-
-def bulk_kernel(x_ref, g1, g2, g3, up_ref, down_ref, far_ref, even, odd, halo1, halo2):
+            yield (count, offset, k), v
+
+
+def bulk_kernel(odd_ref, x_ref, g1, g2, g3, chip_ref, across_ref, far_ref, even, odd, halo1, halo2):
     def pair(g):
         return lambda t: jnp.concatenate([g[2 * t], g[2 * t + 1]], axis=1)
 
     y_level(lambda t: x_ref[:, pl.ds(256 * t, 256)], 8, None, even, odd, g1, halo1)
     y_level(pair(g1), 4, halo1, even, odd, g2, halo2)
     y_level(pair(g2), 2, halo2, even, odd, g3, None)
-    refs = (up_ref, down_ref, far_ref)
     for count, g in ((1, g1), (2, g2), (3, g3)):
         for t in range(TILES[count]):
             level = block_levels([x_lines(g.at[t], x) for x in range(N)], count)
-            for m, key, v in x_spill(level, count):
-                put(refs[m], X_PLACES[m], key + (t,), v)
+            for key, v, w in x_near(level, count, odd_ref[0] == 0):
+                put(chip_ref, X_NEAR[0], key + (t,), v)
+                put(across_ref, X_NEAR[0], key + (t,), w)
+            for key, v in x_far(level, count):
+                put(far_ref, X_FAR[0], key + (t,), v)
 
 
 def halo_matrix():
@@ -276,7 +281,17 @@
     return jnp.where(keep, value, 0.0)
 
 
-def halo_kernel(above_ref, below_ref, w_ref, up_in, down_in, far_in, d_ref, up_ref, down_ref, far_ref, halo):
+def add_edges(out, ins, places, key, value):
+    turned = pltpu.roll(value, 64, 1)
+    for t in range(TILES[key[0]]):
+        own = ins[pl.ds(places[key + (t,)], N), :]
+        put(out, places, key + (t,), plus(own, edges(key[0], t, value, turned)))
+
+
+EDGE = {key: N * at for at, key in enumerate(sorted({key[:3] for key in X_NEAR[0]}))}
+
+
+def halo_kernel(odd_ref, above_ref, below_ref, w_ref, chip_in, far_in, d_ref, chip_ref, edge_ref, far_ref, halo):
     lane = lax.broadcasted_iota(jnp.int32, (64, 128), 1)
     for g in range(4):
         a, b = above_ref[...], below_ref[...]
@@ -286,14 +301,13 @@
     both = jnp.dot(halo[...], w_ref[...], precision=lax.Precision.HIGHEST, preferred_element_type=F32)
     for c in range(3):
         d_ref[c] = both[:, 128 * c : 128 * c + 128]
-    ins, refs = (up_in, down_in, far_in), (up_ref, down_ref, far_ref)
     for count in ALL:
         level = block_levels([x_lines(d_ref.at[count - 1], x) for x in range(N)], count)
-        for m, key, v in x_spill(level, count):
-            turned = pltpu.roll(v, 64, 1)
-            for t in range(TILES[count]):
-                own = ins[m][pl.ds(X_PLACES[m][key + (t,)], N), :]
-                put(refs[m], X_PLACES[m], key + (t,), plus(own, edges(count, t, v, turned)))
+        for key, v, w in x_near(level, count, odd_ref[0] == 0):
+            add_edges(chip_ref, chip_in, X_NEAR[0], key, v)
+            edge_ref[pl.ds(EDGE[key], N), :] = w
+        for key, v in x_far(level, count):
+            add_edges(far_ref, far_in, X_FAR[0], key, v)
 
 
 def own_x_kernel(g1, g2, g3, d_ref, o1, o2, o3):
@@ -316,7 +330,7 @@
             continue
 
         def line(k, offset=offset, places=places, ref=ref):
-            return ref[pl.ds(places[count, offset, k, t], height), :]
+            return ref(pl.ds(places[count, offset, k, t], height))
 
         lines = [functools.partial(line, k) for k in range(len(PLAN[count][offset][0]))]
         total = plus(total, added(count, offset, row, lines))
@@ -327,9 +341,26 @@
     return [g[t, pl.ds(z, 2 * own_count(count), stride=N), :] for z in range(N)]
 
 
-def x_kernel(i1, i2, i3, up_in, down_in, far_in, o1, o2, o3, up_ref, down_ref, up2_ref, down2_ref):
-    near = [(1, X_UP[0], up_in), (-1, X_DOWN[0], down_in)]
-    far = [(2, X_FAR[0], far_in), (-2, X_FAR[0], far_in)]
+def rows_of(ref):
+    return lambda rows: ref[rows, :]
+
+
+def x_kernel(
+    odd_ref, i1, i2, i3, chip_in, across_in, edge_in, far_in, o1, o2, o3, up_ref, down_ref, up2_ref, down2_ref, below, above
+):
+    even = odd_ref[0] == 0
+    for key, at in EDGE.items():
+        line = edge_in[pl.ds(at, N), :]
+        turned = pltpu.roll(line, 64, 1)
+        for t in range(TILES[key[0]]):
+            rows = pl.ds(X_NEAR[0][key + (t,)], N)
+            across = plus(across_in[rows, :], edges(key[0], t, line, turned))
+            chip = chip_in[rows, :]
+            below[rows, :] = jnp.where(even, across, chip)
+            above[rows, :] = jnp.where(even, chip, across)
+    places = {**X_NEAR[0], **{(c, -1, k, t): at for (c, _, k, t), at in X_NEAR[0].items()}}
+    near = [(1, places, rows_of(below)), (-1, places, rows_of(above))]
+    far = [(2, X_FAR[0], rows_of(far_in)), (-2, X_FAR[0], rows_of(far_in))]
     for count, own, g in ((1, i1, o1), (2, i2, o2), (3, i3, o3)):
         n = own_count(count)
         sources = near + far if count == 3 else near
@@ -359,25 +390,43 @@
                     o[t, b * n + i] = level.get(band, i)
 
 
-def z_kernel(i1, i2, i3, up_in, down_in, up2_in, down2_in, one_ref, two_ref, three_ref, last_ref):
-    near = [(1, Z_UP[0], up_in), (-1, Z_DOWN[0], down_in)]
-    far = [(2, Z_UP2[0], up2_in), (-2, Z_DOWN2[0], down2_in)]
-    for count, g, o in ((1, i1, one_ref), (2, i2, two_ref), (3, i3, three_ref)):
+def z_kernel(i1, i2, i3, up_in, down_in, up2_in, down2_in, one_hbm, two_hbm, three_hbm, last_hbm, one, two, three, last, sems):
+    near = [(1, Z_UP[0], rows_of(up_in)), (-1, Z_DOWN[0], rows_of(down_in))]
+    far = [(2, Z_UP2[0], rows_of(up2_in)), (-2, Z_DOWN2[0], rows_of(down2_in))]
+    leaving = []
+
+    def leave(source, target):
+        copy = pltpu.make_async_copy(source, target, sems.at[len(leaving)])
+        copy.start()
+        leaving.append(copy)
+
+    for count, g, o, hbm in ((1, i1, one, one_hbm), (2, i2, two, two_hbm), (3, i3, three, three_hbm)):
         n = own_count(count)
         sources = near + far if count == 3 else near
-        for t in range(TILES[count]):
-            hy, tile = divmod(t, TILES[count] // 2)
-            lanes = pl.ds(128 * tile, 128)
-            for row in range(2 * n):
-                hz, z = divmod(row, n)
-                value = plus(g[t, row], received(count, row, t, 2 * n, sources))
-                for hx in range(2):
-                    part = value[hx * n : hx * n + n]
-                    band = hz * 4 + hy * 2 + hx
-                    if band:
-                        o[band - 1, z, :, lanes] = part
-                    elif count == 3:
-                        last_ref[z, :, lanes] = part
+        half = TILES[count] // 2
+        for hz in range(2):
+            for hy in range(2):
+                for t in range(hy * half, hy * half + half):
+                    lanes = pl.ds(128 * (t - hy * half), 128)
+                    for z in range(n):
+                        row = hz * n + z
+                        value = plus(g[t, row], received(count, row, t, 2 * n, sources))
+                        for hx in range(2):
+                            part = value[hx * n : hx * n + n]
+                            band = hz * 4 + hy * 2 + hx
+                            if band:
+                                o[band - 1, z, :, lanes] = part
+                            elif count == 3:
+                                last[z, :, lanes] = part
+                if count == 1:
+                    first = max(hz * 4 + hy * 2, 1) - 1
+                    bands = pl.ds(first, hz * 4 + hy * 2 + 1 - first)
+                    leave(o.at[bands], hbm.at[bands])
+        if count > 1:
+            leave(o, hbm)
+    leave(last, last_hbm)
+    for copy in leaving:
+        copy.wait()
 
 
 VMEM = pl.BlockSpec(memory_space=pltpu.VMEM)
@@ -392,12 +441,15 @@
     return [pltpu.with_memory_space_constraint(a, space) for a in arrays]
 
 
-def call(kernel, arrays, out_shape, name, scratch=(), moved=4):
+def call(kernel, arrays, out_shape, name, scratch=(), moved=4, odd=None):
     arrays = pinned(arrays)
+    specs = [VMEM] * len(arrays)
+    if odd is not None:
+        arrays, specs = [odd, *arrays], [pl.BlockSpec(memory_space=pltpu.SMEM), *specs]
     return pl.pallas_call(
         kernel,
         out_shape=out_shape,
-        in_specs=[VMEM] * len(arrays),
+        in_specs=specs,
         out_specs=tuple([VMEM] * len(out_shape)),
         scratch_shapes=scratch,
         compiler_params=PARAMS,
@@ -409,6 +461,12 @@
 def shift(x, axis, by):
     peers = lax.axis_size(axis)
     return lax.ppermute(x, axis, [(i, (i + by) % peers) for i in range(peers)])
+
+
+def swap(x, axis, first):
+    peers = lax.axis_size(axis)
+    pairs = [(i % peers, (i + 1) % peers) for i in range(first, first + peers, 2)]
+    return lax.ppermute(x, axis, pairs + [(b, a) for a, b in pairs])
 
 
 def on_device(density):
@@ -427,23 +485,27 @@
     below = shift(to_up, "gy", 1)
 
     rows = {c: 2 * own_count(c) for c in ALL}
-    messages = in_vmem(*[(m[1], 128) for m in (X_UP, X_DOWN, X_FAR)])
-    outs = in_vmem(*[(TILES[c], 256, 128) for c in ALL]) + messages
+    odd = (lax.axis_index("gx") % 2).astype(jnp.int32).reshape(1)
+    near, edge, far = in_vmem((X_NEAR[1], 128), (N * len(EDGE), 128), (X_FAR[1], 128))
+    outs = in_vmem(*[(TILES[c], 256, 128) for c in ALL]) + (near, near, far)
     scratch = in_vmem((256, 640), (256, 640), (256, 128), (256, 128))
-    g1, g2, g3, up, down, far = call(bulk_kernel, (flat,), outs, "own_y", scratch, 12)
-    outs = in_vmem((3, 256, 128)) + messages
+    g1, g2, g3, chip, across, far_own = call(bulk_kernel, (flat,), outs, "own_y", scratch, 12, odd)
+    across = swap(across, "gx", 1)
     weights = jnp.asarray(halo_matrix())
-    d, up, down, far = call(
-        halo_kernel, (above, below, weights, up, down, far), outs, "halo_y", in_vmem((256, 128))
+    outs = in_vmem((3, 256, 128)) + (near, edge, far)
+    d, chip, edge, far = call(
+        halo_kernel, (above, below, weights, chip, far_own), outs, "halo_y", in_vmem((256, 128)), 4, odd
     )
-    up = shift(up, "gx", 1)
-    down = shift(down, "gx", -1)
+    edge = swap(edge, "gx", 1)
+    chip = swap(chip, "gx", 0)
     far = shift(far, "gx", 2)
 
     blocks = in_vmem(*[(TILES[c], rows[c] * N, 128) for c in ALL])
     own = call(own_x_kernel, (g1, g2, g3, d), blocks, "own_x", (), 8)
     outs = blocks + in_vmem(*[(m[1], 128) for m in (Z_UP, Z_DOWN, Z_UP2, Z_DOWN2)])
-    a1, a2, a3, up, down, up2, down2 = call(x_kernel, (*own, up, down, far), outs, "spill_x")
+    a1, a2, a3, up, down, up2, down2 = call(
+        x_kernel, (*own, chip, across, edge, far), outs, "spill_x", (near, near), 4, odd
+    )
     up = shift(up, "gz", 1)
     down = shift(down, "gz", -1)
     up2 = shift(up2, "gz", 2)
@@ -451,10 +513,16 @@
 
     outs = in_vmem(*[(TILES[c], rows[c], rows[c], 128) for c in ALL])
     own = call(own_z_kernel, (a1, a2, a3), outs, "own_z", (), 8)
-    outs = tuple(
-        jax.ShapeDtypeStruct(s, F32) for s in ((7, 8, 8, 512), (7, 4, 4, 256), (7, 2, 2, 128), (2, 2, 128))
-    )
-    return call(z_kernel, (*own, up, down, up2, down2), outs, "spill_z")
+    shapes = ((7, 8, 8, 512), (7, 4, 4, 256), (7, 2, 2, 128), (2, 2, 128))
+    return pl.pallas_call(
+        z_kernel,
+        out_shape=tuple(jax.ShapeDtypeStruct(shape, F32) for shape in shapes),
+        in_specs=[VMEM] * 7,
+        out_specs=tuple([pl.BlockSpec(memory_space=pltpu.HBM)] * 4),
+        scratch_shapes=[*in_vmem(*shapes), pltpu.SemaphoreType.DMA((7,))],
+        compiler_params=PARAMS,
+        name="spill_z",
+    )(*pinned((*own, up, down, up2, down2)))
 
 
 def solution(mesh):

time: 56.4 us -> 55.6 us (0.986)
  the two profiles are of different devices: /device:TPU:8 before, /device:TPU:48 now
where the time goes in v3:
time: 55.6 us; the launch traced here: 55.2 us
  starting transfers between devices  42.3 us (76%)
  Pallas kernels  9.38 us (17%)
  waiting for transfers between devices  2.73 us (5%)
  between operations  0.81 us (1%)
    ppermute x7, starting transfers between devices, shift(): return lax.ppermute(x, axis, [(i, (i + by) % peers) for i in range(peers)])  34.8 us
    ppermute x3, starting transfers between devices, swap(): return lax.ppermute(x, axis, pairs + [(b, a) for a, b in pairs])  7.48 us
    pallas_call x5, Pallas kernels, call(): pl.pallas_call(kernel, out_shape=out_shape, in_specs=specs, out_specs=tup...  7.17 us
    ppermute x7, waiting for transfers between devices, shift(): return lax.ppermute(x, axis, [(i, (i + by) % peers) for i in range(peers)])  2.72 us
    pallas_call x1, Pallas kernels, on_device(): pl.pallas_call(pack_kernel, grid=(1,), out_shape=in_vmem((64, 128), (64,...  1.17 us
  transfers between devices with their start and end apart: 10, of which 2 were waited for; matrix products, arithmetic and copies ran while one was open for 0% of the time, Pallas kernels for 12%

profile of v3, /device:TPU:48, one launch (start us, length us, event | category | flops | bytes accessed | tf_op | source)
XLA Modules:
  0.0 55.2 jit_solution(347975543163384044)
XLA Ops:
  0.6 0.0 copy-start
  0.6 1.2 %pack_y.1 = (f32[64,128]{1,0:T(8,128)S(1)}, f32[64,128]{1,0:T(8,128)S(1)}) custom-call(f32[256,1024]{1,0:T(8,128)} %bitcast.2, f32[256,1024]{1,0:T(8,128)} %bitcast.3), custom_call_target="tpu_custom_call" | custom-call | tf_op jit(solution)/shard_map/pack_y/pallas_call | solution.py:475
  1.8 4.0 %collective-permute-start = (f32[64,128]{1,0:T(8,128)S(1)}, f32[64,128]{1,0:T(8,128)S(1)}, u32[]{:S(2)}, u32[]{:S(2)}) collective-permute-start(f32[64,128]{1,0:T(8,128)S(1)} %get-tuple-element.32), channel_id=1, source_target_pairs={{0,96},{32,0},{64,32},{96,64},{1,97},{33,1},{65,33},{97,65},{2,98}... | collective-permute-start | bytes 98312 | tf_op jit(solution)/shard_map/ppermute | solution.py:463
  5.9 5.0 %collective-permute-start.1 = (f32[64,128]{1,0:T(8,128)S(1)}, f32[64,128]{1,0:T(8,128)S(1)}, u32[]{:S(2)}, u32[]{:S(2)}) collective-permute-start(f32[64,128]{1,0:T(8,128)S(1)} %get-tuple-element.33), channel_id=1, source_target_pairs={{0,32},{32,64},{64,96},{96,0},{1,33},{33,65},{65,97},{97,1},{2,34}... | collective-permute-start | bytes 98312 | tf_op jit(solution)/shard_map/ppermute | solution.py:463
  10.9 0.0 copy-done
  10.9 0.0 copy-start.1
  11.0 3.4 %own_y.1 = (f32[8,256,128]{2,1,0:T(8,128)S(1)}, f32[4,256,128]{2,1,0:T(8,128)S(1)}, f32[2,256,128]{2,1,0:T(8,128)S(1)}, f32[576,128]{1,0:T(8,128)S(1)}, f32[576,128]{1,0:T(8,128)S(1)}, /*index=5*/f32[96,128]{1,0:T(8,128)S(1)}) custom-call(s32[1]{0:T(128)} %bitcast.odd_ref, f32[256,1024]{1,0:T(8,128)S(1)} %bitcast.4), custom_call_target="tpu_custom_call" | custom-call | bytes 12582912 | tf_op jit(solution)/shard_map/own_y/pallas_call | solution.py:449
  14.3 1.9 %collective-permute-start.3 = (f32[576,128]{1,0:T(8,128)S(1)}, f32[576,128]{1,0:T(8,128)S(1)}, u32[]{:S(2)}, u32[]{:S(2)}) collective-permute-start(f32[576,128]{1,0:T(8,128)S(1)} %get-tuple-element.41), channel_id=1, source_target_pairs={{128,256},{384,0},{256,128},{0,384},{129,257},{385,1},{257,129},{1... | collective-permute-start | bytes 884744 | tf_op jit(solution)/shard_map/ppermute | solution.py:469
  16.3 0.0 collective-permute-done.above_ref
  16.3 0.0 collective-permute-done.1.below_ref
  16.3 0.0 copy-done.1
  16.3 0.8 %halo_y.1 = (f32[3,256,128]{2,1,0:T(8,128)S(1)}, f32[576,128]{1,0:T(8,128)S(1)}, f32[144,128]{1,0:T(8,128)S(1)}, f32[96,128]{1,0:T(8,128)S(1)}) custom-call(s32[1]{0:T(128)} %bitcast.odd_ref, f32[64,128]{1,0:T(8,128)S(1)} %collective-permute-done.above_ref, f32[64,128]{1,0:T(8,128)S(1)} %collective-permute-done.1.below_ref, f32[128,384]{1,0:T(8,128)S(1)} %copy-done.1, ...), custom_call_target="tpu_custom_call" | custom-call | bytes 4194304 | tf_op jit(solution)/shard_map/halo_y/pallas_call | solution.py:449
  17.1 1.9 %collective-permute-start.2 = (f32[576,128]{1,0:T(8,128)S(1)}, f32[576,128]{1,0:T(8,128)S(1)}, u32[]{:S(2)}, u32[]{:S(2)}) collective-permute-start(f32[576,128]{1,0:T(8,128)S(1)} %get-tuple-element.40), channel_id=1, source_target_pairs={{0,128},{256,384},{128,0},{384,256},{1,129},{257,385},{129,1},{385... | collective-permute-start | bytes 884744 | tf_op jit(solution)/shard_map/ppermute | solution.py:469
  19.1 3.6 %collective-permute-start.4 = (f32[144,128]{1,0:T(8,128)S(1)}, f32[144,128]{1,0:T(8,128)S(1)}, u32[]{:S(2)}, u32[]{:S(2)}) collective-permute-start(f32[144,128]{1,0:T(8,128)S(1)} %get-tuple-element.42), channel_id=1, source_target_pairs={{128,256},{384,0},{256,128},{0,384},{129,257},{385,1},{257,129},{1... | collective-permute-start | bytes 221192 | tf_op jit(solution)/shard_map/ppermute | solution.py:469
  22.7 2.3 %collective-permute-start.5 = (f32[96,128]{1,0:T(8,128)S(1)}, f32[96,128]{1,0:T(8,128)S(1)}, u32[]{:S(2)}, u32[]{:S(2)}) collective-permute-start(f32[96,128]{1,0:T(8,128)S(1)} %get-tuple-element.43), channel_id=1, source_target_pairs={{0,256},{128,384},{256,0},{384,128},{1,257},{129,385},{257,1},{385... | collective-permute-start | bytes 147464 | tf_op jit(solution)/shard_map/ppermute | solution.py:463
  25.0 1.6 %own_x.1 = (f32[8,256,128]{2,1,0:T(8,128)S(1)}, f32[4,128,128]{2,1,0:T(8,128)S(1)}, f32[2,64,128]{2,1,0:T(8,128)S(1)}) custom-call(f32[8,256,128]{2,1,0:T(8,128)S(1)} %get-tuple-element.29.g1, f32[4,256,128]{2,1,0:T(8,128)S(1)} %get-tuple-element.30.g2, f32[2,256,128]{2,1,0:T(8,128)S(1)} %get-tuple-element.31.g3, f32[3,256,128]{2,1,0:T(8,128)S(1)} %get-tuple-element.36.d_ref), custom_call_target="tpu_custom_call" | custom-call | bytes 8388608 | tf_op jit(solution)/shard_map/own_x/pallas_call | solution.py:449
  26.6 2.1 %collective-permute-done.5.far_in = f32[96,128]{1,0:T(8,128)S(1)} collective-permute-done((f32[96,128]{1,0:T(8,128)S(1)}, f32[96,128]{1,0:T(8,128)S(1)}, u32[]{:S(2)}, u32[]{:S(2)}) %collective-permute-start.5) | collective-permute-done | bytes 49184 | tf_op jit(solution)/shard_map/ppermute | solution.py:463
  28.7 0.0 collective-permute-done.4.edge_in
  28.7 0.0 collective-permute-done.3.across_in
  28.8 0.0 collective-permute-done.2.chip_in
  28.8 0.6 %spill_x.1 = (f32[8,256,128]{2,1,0:T(8,128)S(1)}, f32[4,128,128]{2,1,0:T(8,128)S(1)}, f32[2,64,128]{2,1,0:T(8,128)S(1)}, f32[384,128]{1,0:T(8,128)S(1)}, f32[376...) custom-call(s32[1]{0:T(128)} %bitcast.odd_ref, f32[8,256,128]{2,1,0:T(8,128)S(1)} %get-tuple-element.37.i1, ...), custom_call_target="tpu_custom_call" | custom-call | bytes 4194304 | tf_op jit(solution)/shard_map/spill_x/pallas_call | solution.py:449
  29.4 2.3 %collective-permute-start.6 = (f32[384,128]{1,0:T(8,128)S(1)}, f32[384,128]{1,0:T(8,128)S(1)}, u32[]{:S(2)}, u32[]{:S(2)}) collective-permute-start(f32[384,128]{1,0:T(8,128)S(1)} %get-tuple-element.50), channel_id=1, source_target_pairs={{0,1},{1,2},{2,3},{3,4},{4,5},{5,6},{6,7},{7,8},{8,9},{9,10},{10,1... | collective-permute-start | bytes 589832 | tf_op jit(solution)/shard_map/ppermute | solution.py:463
  31.7 11.7 %collective-permute-start.7 = (f32[376,128]{1,0:T(8,128)S(1)}, f32[376,128]{1,0:T(8,128)S(1)}, u32[]{:S(2)}, u32[]{:S(2)}) collective-permute-start(f32[376,128]{1,0:T(8,128)S(1)} %get-tuple-element.51), channel_id=1, source_target_pairs={{0,31},{1,0},{2,1},{3,2},{4,3},{5,4},{6,5},{7,6},{8,7},{9,8},{10,9... | collective-permute-start | bytes 577544 | tf_op jit(solution)/shard_map/ppermute | solution.py:463
  43.4 1.9 %collective-permute-start.8 = (f32[16,128]{1,0:T(8,128)S(1)}, f32[16,128]{1,0:T(8,128)S(1)}, u32[]{:S(2)}, u32[]{:S(2)}) collective-permute-start(f32[16,128]{1,0:T(8,128)S(1)} %get-tuple-element.52), channel_id=1, source_target_pairs={{0,2},{1,3},{2,4},{3,5},{4,6},{5,7},{6,8},{7,9},{8,10},{9,11},{10,... | collective-permute-start | bytes 24584 | tf_op jit(solution)/shard_map/ppermute | solution.py:463
  45.3 7.5 %collective-permute-start.9 = (f32[8,128]{1,0:T(8,128)S(1)}, f32[8,128]{1,0:T(8,128)S(1)}, u32[]{:S(2)}, u32[]{:S(2)}) collective-permute-start(f32[8,128]{1,0:T(8,128)S(1)} %get-tuple-element.53), channel_id=1, source_target_pairs={{0,30},{1,31},{2,0},{3,1},{4,2},{5,3},{6,4},{7,5},{8,6},{9,7},{10,... | collective-permute-start | bytes 12296 | tf_op jit(solution)/shard_map/ppermute | solution.py:463
  52.8 0.7 %own_z.1 = (f32[8,16,16,128]{3,2,1,0:T(8,128)S(1)}, f32[4,8,8,128]{3,2,1,0:T(8,128)S(1)}, f32[2,4,4,128]{3,2,1,0:T(4,128)S(1)}) custom-call(f32[8,256,128]{2,1,0:T(8,128)S(1)} %get-tuple-element.44.g1, f32[4,128,128]{2,1,0:T(8,128)S(1)} %get-tuple-element.45.g2, f32[2,64,128]{2,1,0:T(8,128)S(1)} %get-tuple-element.46.g3), custom_call_target="tpu_custom_call" | custom-call | bytes 8388608 | tf_op jit(solution)/shard_map/own_z/pallas_call | solution.py:449
  53.6 0.6 %collective-permute-done.9.down2_in = f32[8,128]{1,0:T(8,128)S(1)} collective-permute-done((f32[8,128]{1,0:T(8,128)S(1)}, f32[8,128]{1,0:T(8,128)S(1)}, u32[]{:S(2)}, u32[]{:S(2)}) %collective-permute-start.9) | collective-permute-done | bytes 4128 | tf_op jit(solution)/shard_map/ppermute | solution.py:463
  54.1 0.0 collective-permute-done.8.up2_in
  54.1 0.0 collective-permute-done.7.down_in
  54.1 0.0 collective-permute-done.6.up_in
  54.1 1.0 %spill_z.1 = (f32[7,8,8,512]{3,2,1,0:T(8,128)}, f32[7,4,4,256]{3,2,1,0:T(4,128)}, f32[7,2,2,128]{3,2,1,0:T(2,128)}, f32[2,2,128]{2,1,0:T(2,128)}) custom-call(f32[8,16,16,128]{3,2,1,0:T(8,128)S(1)} %get-tuple-element.47.i1, f32[4,8,8,128]{3,2,1,0:T(8,128)S(1)} %get-tuple-element.48.i2, f32[2,4,4,128]{3,2,1,0:T(4,128)S(1)} %get-tuple-element.49.i3, ...), custom_call_target="tpu_custom_call" | custom-call | tf_op jit(solution)/shard_map/spill_z/pallas_call | solution.py:517
Async XLA Ops:
  0.6 10.3 %copy-start = (f32[16,16,1024]{2,1,0:T(8,128)S(1)}, f32[16,16,1024]{2,1,0:T(8,128)}, u32[]{:S(2)}) copy-start(f32[16,16,1024]{2,1,0:T(8,128)} %param.2) | copy-start | bytes 3145732
  1.8 14.5 %collective-permute-start = (f32[64,128]{1,0:T(8,128)S(1)}, f32[64,128]{1,0:T(8,128)S(1)}, u32[]{:S(2)}, u32[]{:S(2)}) collective-permute-start(f32[64,128]{1,0:T(8,128)S(1)} %get-tuple-element.32), channel_id=1, source_target_pairs={{0,96},{32,0},{64,32},{96,64},{1,97},{33,1},{65,33},{97,65},{2,98}... | collective-permute-start | bytes 98312 | tf_op jit(solution)/shard_map/ppermute | solution.py:463
  5.9 10.4 %collective-permute-start.1 = (f32[64,128]{1,0:T(8,128)S(1)}, f32[64,128]{1,0:T(8,128)S(1)}, u32[]{:S(2)}, u32[]{:S(2)}) collective-permute-start(f32[64,128]{1,0:T(8,128)S(1)} %get-tuple-element.33), channel_id=1, source_target_pairs={{0,32},{32,64},{64,96},{96,0},{1,33},{33,65},{65,97},{97,1},{2,34}... | collective-permute-start | bytes 98312 | tf_op jit(solution)/shard_map/ppermute | solution.py:463
  10.9 5.4 %copy-start.1 = (f32[128,384]{1,0:T(8,128)S(1)}, f32[128,384]{1,0:T(8,128)}, u32[]{:S(2)}) copy-start(f32[128,384]{1,0:T(8,128)} %constant.21.clone.w_ref) | copy-start | bytes 589828
  14.3 14.4 %collective-permute-start.3 = (f32[576,128]{1,0:T(8,128)S(1)}, f32[576,128]{1,0:T(8,128)S(1)}, u32[]{:S(2)}, u32[]{:S(2)}) collective-permute-start(f32[576,128]{1,0:T(8,128)S(1)} %get-tuple-element.41), channel_id=1, source_target_pairs={{128,256},{384,0},{256,128},{0,384},{129,257},{385,1},{257,129},{1... | collective-permute-start | bytes 884744 | tf_op jit(solution)/shard_map/ppermute | solution.py:469
  17.1 11.6 %collective-permute-start.2 = (f32[576,128]{1,0:T(8,128)S(1)}, f32[576,128]{1,0:T(8,128)S(1)}, u32[]{:S(2)}, u32[]{:S(2)}) collective-permute-start(f32[576,128]{1,0:T(8,128)S(1)} %get-tuple-element.40), channel_id=1, source_target_pairs={{0,128},{256,384},{128,0},{384,256},{1,129},{257,385},{129,1},{385... | collective-permute-start | bytes 884744 | tf_op jit(solution)/shard_map/ppermute | solution.py:469
  19.1 9.7 %collective-permute-start.4 = (f32[144,128]{1,0:T(8,128)S(1)}, f32[144,128]{1,0:T(8,128)S(1)}, u32[]{:S(2)}, u32[]{:S(2)}) collective-permute-start(f32[144,128]{1,0:T(8,128)S(1)} %get-tuple-element.42), channel_id=1, source_target_pairs={{128,256},{384,0},{256,128},{0,384},{129,257},{385,1},{257,129},{1... | collective-permute-start | bytes 221192 | tf_op jit(solution)/shard_map/ppermute | solution.py:469
  22.7 6.0 %collective-permute-start.5 = (f32[96,128]{1,0:T(8,128)S(1)}, f32[96,128]{1,0:T(8,128)S(1)}, u32[]{:S(2)}, u32[]{:S(2)}) collective-permute-start(f32[96,128]{1,0:T(8,128)S(1)} %get-tuple-element.43), channel_id=1, source_target_pairs={{0,256},{128,384},{256,0},{384,128},{1,257},{129,385},{257,1},{385... | collective-permute-start | bytes 147464 | tf_op jit(solution)/shard_map/ppermute | solution.py:463
  29.4 24.7 %collective-permute-start.6 = (f32[384,128]{1,0:T(8,128)S(1)}, f32[384,128]{1,0:T(8,128)S(1)}, u32[]{:S(2)}, u32[]{:S(2)}) collective-permute-start(f32[384,128]{1,0:T(8,128)S(1)} %get-tuple-element.50), channel_id=1, source_target_pairs={{0,1},{1,2},{2,3},{3,4},{4,5},{5,6},{6,7},{7,8},{8,9},{9,10},{10,1... | collective-permute-start | bytes 589832 | tf_op jit(solution)/shard_map/ppermute | solution.py:463
  31.7 22.5 %collective-permute-start.7 = (f32[376,128]{1,0:T(8,128)S(1)}, f32[376,128]{1,0:T(8,128)S(1)}, u32[]{:S(2)}, u32[]{:S(2)}) collective-permute-start(f32[376,128]{1,0:T(8,128)S(1)} %get-tuple-element.51), channel_id=1, source_target_pairs={{0,31},{1,0},{2,1},{3,2},{4,3},{5,4},{6,5},{7,6},{8,7},{9,8},{10,9... | collective-permute-start | bytes 577544 | tf_op jit(solution)/shard_map/ppermute | solution.py:463
  43.4 10.8 %collective-permute-start.8 = (f32[16,128]{1,0:T(8,128)S(1)}, f32[16,128]{1,0:T(8,128)S(1)}, u32[]{:S(2)}, u32[]{:S(2)}) collective-permute-start(f32[16,128]{1,0:T(8,128)S(1)} %get-tuple-element.52), channel_id=1, source_target_pairs={{0,2},{1,3},{2,4},{3,5},{4,6},{5,7},{6,8},{7,9},{8,10},{9,11},{10,... | collective-permute-start | bytes 24584 | tf_op jit(solution)/shard_map/ppermute | solution.py:463
  45.3 8.8 %collective-permute-start.9 = (f32[8,128]{1,0:T(8,128)S(1)}, f32[8,128]{1,0:T(8,128)S(1)}, u32[]{:S(2)}, u32[]{:S(2)}) collective-permute-start(f32[8,128]{1,0:T(8,128)S(1)} %get-tuple-element.53), channel_id=1, source_target_pairs={{0,30},{1,31},{2,0},{3,1},{4,2},{5,3},{6,4},{7,5},{8,6},{9,7},{10,... | collective-permute-start | bytes 12296 | tf_op jit(solution)/shard_map/ppermute | solution.py:463

commit v4 on v3

--- a/solution.py
+++ b/solution.py
@@ -174,40 +174,30 @@
     return (dot(lo, selection) + dot(mid, selection)) + dot(hi, selection)
 
 
-def y_level(source, tiles, halo, even, odd, out, low_halo):
+def y_level(source, tiles, even, odd, out):
     half = tiles // 2
-    width = half * 128 + 128
+    width = half * 128
     i = lax.broadcasted_iota(jnp.int32, (256, 256), 0)
     j = lax.broadcasted_iota(jnp.int32, (256, 256), 1)
     pick = (i == 2 * (j % 128) + j // 128).astype(jnp.bfloat16)
-    for t in range(half):
-        both = split_dot(source(t), pick)
-        even[:, pl.ds(128 * t, 128)] = both[:, :128]
-        odd[:, pl.ds(128 * t, 128)] = both[:, 128:]
-    if halo is None:
-        both = jnp.zeros((256, 256), F32)
-    else:
-        i = lax.broadcasted_iota(jnp.int32, (128, 256), 0)
-        j = lax.broadcasted_iota(jnp.int32, (128, 256), 1)
-        pick_halo = (i == (2 * (j % 128) + j // 128) % 128).astype(jnp.bfloat16)
-        both = split_dot(halo[...], pick_halo)
-    even[:, pl.ds(128 * half, 128)] = both[:, :128]
-    odd[:, pl.ds(128 * half, 128)] = both[:, 128:]
-    chunk = 16
-    for r in range(0, 256, chunk):
-        rows = pl.ds(r, chunk)
-        s, d = even[rows, :width], odd[rows, :width]
-        ahead = lambda v: pltpu.roll(v, width - 1, 1)
-        behind = lambda v: pltpu.roll(v, 1, 1)
-        d = d + ALPHA * (s + ahead(s))
-        s = s + BETA * (behind(d) + d)
-        d = d + GAMMA * (s + ahead(s))
-        s = s + DELTA * (behind(d) + d)
+    for block in range(0, 256, 128):
+        rows = pl.ds(block, 128)
         for t in range(half):
-            out[t, rows, :] = s[:, 128 * t : 128 * t + 128] * ZETA
-            out[half + t, rows, :] = d[:, 128 * t : 128 * t + 128] * (1.0 / ZETA)
-        if low_halo is not None:
-            low_halo[rows, :] = s[:, 128 * half :] * ZETA
+            both = split_dot(source(t, rows), pick)
+            even[rows, pl.ds(128 * t, 128)] = both[:, :128]
+            odd[rows, pl.ds(128 * t, 128)] = both[:, 128:]
+        for r in range(block, block + 128, 16):
+            rows = pl.ds(r, 16)
+            s, d = even[rows, :width], odd[rows, :width]
+            ahead = lambda v: pltpu.roll(v, width - 1, 1)
+            behind = lambda v: pltpu.roll(v, 1, 1)
+            d = d + ALPHA * (s + ahead(s))
+            s = s + BETA * (behind(d) + d)
+            d = d + GAMMA * (s + ahead(s))
+            s = s + DELTA * (behind(d) + d)
+            for t in range(half):
+                out[t, rows, :] = s[:, 128 * t : 128 * t + 128] * ZETA
+                out[half + t, rows, :] = d[:, 128 * t : 128 * t + 128] * (1.0 / ZETA)
 
 
 def put(ref, places, key, value):
@@ -231,14 +221,11 @@
             yield (count, offset, k), v
 
 
-def bulk_kernel(odd_ref, x_ref, g1, g2, g3, chip_ref, across_ref, far_ref, even, odd, halo1, halo2):
+def bulk_kernel(odd_ref, x_ref, g1, g2, g3, chip_ref, across_ref, far_ref, even, odd):
     def pair(g):
-        return lambda t: jnp.concatenate([g[2 * t], g[2 * t + 1]], axis=1)
-
-    y_level(lambda t: x_ref[:, pl.ds(256 * t, 256)], 8, None, even, odd, g1, halo1)
-    y_level(pair(g1), 4, halo1, even, odd, g2, halo2)
-    y_level(pair(g2), 2, halo2, even, odd, g3, None)
-    for count, g in ((1, g1), (2, g2), (3, g3)):
+        return lambda t, rows: jnp.concatenate([g[2 * t, rows, :], g[2 * t + 1, rows, :]], axis=1)
+
+    def spill(count, g):
         for t in range(TILES[count]):
             level = block_levels([x_lines(g.at[t], x) for x in range(N)], count)
             for key, v, w in x_near(level, count, odd_ref[0] == 0):
@@ -246,6 +233,13 @@
                 put(across_ref, X_NEAR[0], key + (t,), w)
             for key, v in x_far(level, count):
                 put(far_ref, X_FAR[0], key + (t,), v)
+
+    y_level(lambda t, rows: x_ref[rows, pl.ds(256 * t, 256)], 8, even, odd, g1)
+    spill(1, g1)
+    y_level(pair(g1), 4, even, odd, g2)
+    spill(2, g2)
+    y_level(pair(g2), 2, even, odd, g3)
+    spill(3, g3)
 
 
 def halo_matrix():
@@ -291,10 +285,12 @@
 EDGE = {key: N * at for at, key in enumerate(sorted({key[:3] for key in X_NEAR[0]}))}
 
 
-def halo_kernel(odd_ref, above_ref, below_ref, w_ref, chip_in, far_in, d_ref, chip_ref, edge_ref, far_ref, halo):
+def halo_kernel(
+    odd_ref, above_ref, below_ref, first_ref, last_ref, w_ref, chip_in, far_in, d_ref, chip_ref, edge_ref, far_ref, halo
+):
     lane = lax.broadcasted_iota(jnp.int32, (64, 128), 1)
     for g in range(4):
-        a, b = above_ref[...], below_ref[...]
+        a, b = above_ref[...] - first_ref[...], below_ref[...] - last_ref[...]
         a = pltpu.roll(a, 128 - 32 * g, 1) if g else a
         b = pltpu.roll(b, 96 - 32 * g, 1) if g < 3 else b
         halo[pl.ds(64 * g, 64), :] = jnp.where(lane < 32, a, jnp.where(lane >= 96, b, 0.0))
@@ -345,11 +341,23 @@
     return lambda rows: ref[rows, :]
 
 
-def x_kernel(
-    odd_ref, i1, i2, i3, chip_in, across_in, edge_in, far_in, o1, o2, o3, up_ref, down_ref, up2_ref, down2_ref, below, above
-):
+def x_kernel(counts, odd_ref, *refs):
+    refs = list(refs)
+    take = lambda n: [refs.pop(0) for _ in range(n)]
+    ins = take(len(counts))
+    chip_in, across_in, edge_in = take(3)
+    last = counts == (3,)
+    if last:
+        far_in, up_in, down_in = take(3)
+    outs = take(len(counts))
+    up_ref, down_ref = take(2)
+    if last:
+        up2_ref, down2_ref = take(2)
+    below, above = take(2)
     even = odd_ref[0] == 0
     for key, at in EDGE.items():
+        if key[0] not in counts:
+            continue
         line = edge_in[pl.ds(at, N), :]
         turned = pltpu.roll(line, 64, 1)
         for t in range(TILES[key[0]]):
@@ -359,11 +367,14 @@
             below[rows, :] = jnp.where(even, across, chip)
             above[rows, :] = jnp.where(even, chip, across)
     places = {**X_NEAR[0], **{(c, -1, k, t): at for (c, _, k, t), at in X_NEAR[0].items()}}
-    near = [(1, places, rows_of(below)), (-1, places, rows_of(above))]
-    far = [(2, X_FAR[0], rows_of(far_in)), (-2, X_FAR[0], rows_of(far_in))]
-    for count, own, g in ((1, i1, o1), (2, i2, o2), (3, i3, o3)):
+    sources = [(1, places, rows_of(below)), (-1, places, rows_of(above))]
+    if last:
+        sources += [(2, X_FAR[0], rows_of(far_in)), (-2, X_FAR[0], rows_of(far_in))]
+        for taken, ref, message in ((up_in, up_ref, Z_UP), (down_in, down_ref, Z_DOWN)):
+            shared = pl.ds(0, min(at for key, at in message[0].items() if key[0] == 3))
+            ref[shared, :] = taken[shared, :]
+    for count, own, g in zip(counts, ins, outs):
         n = own_count(count)
-        sources = near + far if count == 3 else near
         for t in range(TILES[count]):
             for row in range(2 * n):
                 here = (t, pl.ds(row * N, N), slice(None))
@@ -373,7 +384,7 @@
                 put(up_ref, Z_UP[0], (count, 1, k, t), v)
             for k, v in enumerate(sent(level, count, -1)):
                 put(down_ref, Z_DOWN[0], (count, -1, k, t), v)
-            if count == 3:
+            if last:
                 for k, v in enumerate(sent(level, count, 2)):
                     put(up2_ref, Z_UP2[0], (count, 2, k, t), v)
                 for k, v in enumerate(sent(level, count, -2)):
@@ -390,9 +401,24 @@
                     o[t, b * n + i] = level.get(band, i)
 
 
-def z_kernel(i1, i2, i3, up_in, down_in, up2_in, down2_in, one_hbm, two_hbm, three_hbm, last_hbm, one, two, three, last, sems):
-    near = [(1, Z_UP[0], rows_of(up_in)), (-1, Z_DOWN[0], rows_of(down_in))]
-    far = [(2, Z_UP2[0], rows_of(up2_in)), (-2, Z_DOWN2[0], rows_of(down2_in))]
+def z_values(count, g, sources):
+    n = own_count(count)
+    half = TILES[count] // 2
+    for hz in range(2):
+        for hy in range(2):
+            for t in range(hy * half, hy * half + half):
+                for z in range(n):
+                    row = hz * n + z
+                    value = plus(g[t, row], received(count, row, t, 2 * n, sources))
+                    for hx in range(2):
+                        yield hz * 4 + hy * 2 + hx, z, t - hy * half, value[hx * n : hx * n + n]
+
+
+def z_near(up_in, down_in):
+    return [(1, Z_UP[0], rows_of(up_in)), (-1, Z_DOWN[0], rows_of(down_in))]
+
+
+def z_kernel(i1, i2, up_in, down_in, one_hbm, two_hbm, one, two, sems):
     leaving = []
 
     def leave(source, target):
@@ -400,33 +426,31 @@
         copy.start()
         leaving.append(copy)
 
-    for count, g, o, hbm in ((1, i1, one, one_hbm), (2, i2, two, two_hbm), (3, i3, three, three_hbm)):
-        n = own_count(count)
-        sources = near + far if count == 3 else near
-        half = TILES[count] // 2
-        for hz in range(2):
-            for hy in range(2):
-                for t in range(hy * half, hy * half + half):
-                    lanes = pl.ds(128 * (t - hy * half), 128)
-                    for z in range(n):
-                        row = hz * n + z
-                        value = plus(g[t, row], received(count, row, t, 2 * n, sources))
-                        for hx in range(2):
-                            part = value[hx * n : hx * n + n]
-                            band = hz * 4 + hy * 2 + hx
-                            if band:
-                                o[band - 1, z, :, lanes] = part
-                            elif count == 3:
-                                last[z, :, lanes] = part
-                if count == 1:
-                    first = max(hz * 4 + hy * 2, 1) - 1
-                    bands = pl.ds(first, hz * 4 + hy * 2 + 1 - first)
-                    leave(o.at[bands], hbm.at[bands])
-        if count > 1:
-            leave(o, hbm)
-    leave(last, last_hbm)
+    done = 0
+    for band, z, tile, value in z_values(1, i1, z_near(up_in, down_in)):
+        if band // 2 != done:
+            bands = pl.ds(max(2 * done, 1) - 1, min(2, 2 * done + 1))
+            leave(one.at[bands], one_hbm.at[bands])
+            done = band // 2
+        if band:
+            one[band - 1, z, :, pl.ds(128 * tile, 128)] = value
+    bands = pl.ds(5, 2)
+    leave(one.at[bands], one_hbm.at[bands])
+    for band, z, tile, value in z_values(2, i2, z_near(up_in, down_in)):
+        if band:
+            two[band - 1, z, :, pl.ds(128 * tile, 128)] = value
+    leave(two, two_hbm)
     for copy in leaving:
         copy.wait()
+
+
+def z_last_kernel(i3, up_in, down_in, up2_in, down2_in, three, last):
+    far = [(2, Z_UP2[0], rows_of(up2_in)), (-2, Z_DOWN2[0], rows_of(down2_in))]
+    for band, z, _, value in z_values(3, i3, z_near(up_in, down_in) + far):
+        if band:
+            three[band - 1, z] = value
+        else:
+            last[z] = value
 
 
 VMEM = pl.BlockSpec(memory_space=pltpu.VMEM)
@@ -488,13 +512,19 @@
     odd = (lax.axis_index("gx") % 2).astype(jnp.int32).reshape(1)
     near, edge, far = in_vmem((X_NEAR[1], 128), (N * len(EDGE), 128), (X_FAR[1], 128))
     outs = in_vmem(*[(TILES[c], 256, 128) for c in ALL]) + (near, near, far)
-    scratch = in_vmem((256, 640), (256, 640), (256, 128), (256, 128))
+    scratch = in_vmem((256, 512), (256, 512))
     g1, g2, g3, chip, across, far_own = call(bulk_kernel, (flat,), outs, "own_y", scratch, 12, odd)
     across = swap(across, "gx", 1)
     weights = jnp.asarray(halo_matrix())
     outs = in_vmem((3, 256, 128)) + (near, edge, far)
     d, chip, edge, far = call(
-        halo_kernel, (above, below, weights, chip, far_own), outs, "halo_y", in_vmem((256, 128)), 4, odd
+        halo_kernel,
+        (above, below, to_down, to_up, weights, chip, far_own),
+        outs,
+        "halo_y",
+        in_vmem((256, 128)),
+        4,
+        odd,
     )
     edge = swap(edge, "gx", 1)
     chip = swap(chip, "gx", 0)
@@ -502,9 +532,19 @@
 
     blocks = in_vmem(*[(TILES[c], rows[c] * N, 128) for c in ALL])
     own = call(own_x_kernel, (g1, g2, g3, d), blocks, "own_x", (), 8)
-    outs = blocks + in_vmem(*[(m[1], 128) for m in (Z_UP, Z_DOWN, Z_UP2, Z_DOWN2)])
-    a1, a2, a3, up, down, up2, down2 = call(
-        x_kernel, (*own, chip, across, edge, far), outs, "spill_x", (near, near), 4, odd
+    messages = in_vmem(*[(m[1], 128) for m in (Z_UP, Z_DOWN, Z_UP2, Z_DOWN2)])
+    near_x = (chip, across, edge)
+    a1, a2, up, down = call(
+        functools.partial(x_kernel, (1, 2)), (*own[:2], *near_x), blocks[:2] + messages[:2], "spill_x", (near, near), 6, odd
+    )
+    a3, up, down, up2, down2 = call(
+        functools.partial(x_kernel, (3,)),
+        (own[2], *near_x, far, up, down),
+        blocks[2:] + messages,
+        "spill_x_last",
+        (near, near),
+        1,
+        odd,
     )
     up = shift(up, "gz", 1)
     down = shift(down, "gz", -1)
@@ -514,15 +554,19 @@
     outs = in_vmem(*[(TILES[c], rows[c], rows[c], 128) for c in ALL])
     own = call(own_z_kernel, (a1, a2, a3), outs, "own_z", (), 8)
     shapes = ((7, 8, 8, 512), (7, 4, 4, 256), (7, 2, 2, 128), (2, 2, 128))
-    return pl.pallas_call(
+    one, two = pl.pallas_call(
         z_kernel,
-        out_shape=tuple(jax.ShapeDtypeStruct(shape, F32) for shape in shapes),
-        in_specs=[VMEM] * 7,
-        out_specs=tuple([pl.BlockSpec(memory_space=pltpu.HBM)] * 4),
-        scratch_shapes=[*in_vmem(*shapes), pltpu.SemaphoreType.DMA((7,))],
+        out_shape=tuple(jax.ShapeDtypeStruct(shape, F32) for shape in shapes[:2]),
+        in_specs=[VMEM] * 4,
+        out_specs=tuple([pl.BlockSpec(memory_space=pltpu.HBM)] * 2),
+        scratch_shapes=[*in_vmem(*shapes[:2]), pltpu.SemaphoreType.DMA((5,))],
         compiler_params=PARAMS,
+        cost_estimate=pl.CostEstimate(flops=0, transcendentals=0, bytes_accessed=6 * 2**20),
         name="spill_z",
-    )(*pinned((*own, up, down, up2, down2)))
+    )(*pinned((*own[:2], up, down)))
+    outs = tuple(jax.ShapeDtypeStruct(shape, F32) for shape in shapes[2:])
+    three, last = call(z_last_kernel, (own[2], up, down, up2, down2), outs, "spill_z_last", (), 1)
+    return one, two, three, last
 
 
 def solution(mesh):

time: 55.6 us -> 54.6 us (0.982)
  the two profiles are of different devices: /device:TPU:48 before, /device:TPU:8 now
where the time goes in v4:
time: 54.6 us; the launch traced here: 54.2 us
  starting transfers between devices  42.9 us (79%)
  Pallas kernels  9.26 us (17%)
  waiting for transfers between devices  1.19 us (2%)
  between operations  0.85 us (2%)
    ppermute x7, starting transfers between devices, shift(): return lax.ppermute(x, axis, [(i, (i + by) % peers) for i in range(peers)])  32.5 us
    ppermute x3, starting transfers between devices, swap(): return lax.ppermute(x, axis, pairs + [(b, a) for a, b in pairs])  10.4 us
    pallas_call x7, Pallas kernels, call(): pl.pallas_call(kernel, out_shape=out_shape, in_specs=specs, out_specs=tup...  7.07 us
    ppermute x7, waiting for transfers between devices, shift(): return lax.ppermute(x, axis, [(i, (i + by) % peers) for i in range(peers)])  1.18 us
    pallas_call x1, Pallas kernels, on_device(): pl.pallas_call(pack_kernel, grid=(1,), out_shape=in_vmem((64, 128), (64,...  1.17 us
  transfers between devices with their start and end apart: 10, of which 2 were waited for; matrix products, arithmetic and copies ran while one was open for 0% of the time, Pallas kernels for 13%

profile of v4, /device:TPU:8, one launch (start us, length us, event | category | flops | bytes accessed | tf_op | source)
XLA Modules:
  0.0 54.2 jit_solution(9213624595248214351)
XLA Ops:
  0.6 0.0 copy-start
  0.6 1.2 %pack_y.1 = (f32[64,128]{1,0:T(8,128)S(1)}, f32[64,128]{1,0:T(8,128)S(1)}) custom-call(f32[256,1024]{1,0:T(8,128)} %bitcast.2, f32[256,1024]{1,0:T(8,128)} %bitcast.3), custom_call_target="tpu_custom_call" | custom-call | tf_op jit(solution)/shard_map/pack_y/pallas_call | solution.py:499
  1.8 5.3 %collective-permute-start = (f32[64,128]{1,0:T(8,128)S(1)}, f32[64,128]{1,0:T(8,128)S(1)}, u32[]{:S(2)}, u32[]{:S(2)}) collective-permute-start(f32[64,128]{1,0:T(8,128)S(1)} %get-tuple-element.38.first_ref), channel_id=1, source_target_pairs={{0,96},{32,0},{64,32},{96,64},{1,97},{33,1},{65,33},{97,65},{2,98}... | collective-permute-start | bytes 98312 | tf_op jit(solution)/shard_map/ppermute | solution.py:487
  7.1 1.9 %collective-permute-start.1 = (f32[64,128]{1,0:T(8,128)S(1)}, f32[64,128]{1,0:T(8,128)S(1)}, u32[]{:S(2)}, u32[]{:S(2)}) collective-permute-start(f32[64,128]{1,0:T(8,128)S(1)} %get-tuple-element.39.last_ref), channel_id=1, source_target_pairs={{0,32},{32,64},{64,96},{96,0},{1,33},{33,65},{65,97},{97,1},{2,34}... | collective-permute-start | bytes 98312 | tf_op jit(solution)/shard_map/ppermute | solution.py:487
  9.0 0.0 copy-done
  9.0 0.0 copy-start.1
  9.1 2.7 %own_y.1 = (f32[8,256,128]{2,1,0:T(8,128)S(1)}, f32[4,256,128]{2,1,0:T(8,128)S(1)}, f32[2,256,128]{2,1,0:T(8,128)S(1)}, f32[576,128]{1,0:T(8,128)S(1)}, f32[576,128]{1,0:T(8,128)S(1)}, /*index=5*/f32[96,128]{1,0:T(8,128)S(1)}) custom-call(s32[1]{0:T(128)} %bitcast.odd_ref, f32[256,1024]{1,0:T(8,128)S(1)} %bitcast.4), custom_call_target="tpu_custom_call" | custom-call | bytes 12582912 | tf_op jit(solution)/shard_map/own_y/pallas_call | solution.py:473
  11.7 2.4 %collective-permute-start.3 = (f32[576,128]{1,0:T(8,128)S(1)}, f32[576,128]{1,0:T(8,128)S(1)}, u32[]{:S(2)}, u32[]{:S(2)}) collective-permute-start(f32[576,128]{1,0:T(8,128)S(1)} %get-tuple-element.46), channel_id=1, source_target_pairs={{128,256},{384,0},{256,128},{0,384},{129,257},{385,1},{257,129},{1... | collective-permute-start | bytes 884744 | tf_op jit(solution)/shard_map/ppermute | solution.py:493
  14.1 0.0 collective-permute-done.above_ref
  14.2 0.9 %collective-permute-done.1.below_ref = f32[64,128]{1,0:T(8,128)S(1)} collective-permute-done((f32[64,128]{1,0:T(8,128)S(1)}, f32[64,128]{1,0:T(8,128)S(1)}, u32[]{:S(2)}, u32[]{:S(2)}) %collective-permute-start.1) | collective-permute-done | bytes 32800 | tf_op jit(solution)/shard_map/ppermute | solution.py:487
  15.0 0.0 copy-done.1
  15.0 0.8 %halo_y.1 = (f32[3,256,128]{2,1,0:T(8,128)S(1)}, f32[576,128]{1,0:T(8,128)S(1)}, f32[144,128]{1,0:T(8,128)S(1)}, f32[96,128]{1,0:T(8,128)S(1)}) custom-call(s32[1]{0:T(128)} %bitcast.odd_ref, f32[64,128]{1,0:T(8,128)S(1)} %collective-permute-done.above_ref, f32[64,128]{1,0:T(8,128)S(1)} %collective-permute-done.1.below_ref, ...), custom_call_target="tpu_custom_call" | custom-call | bytes 4194304 | tf_op jit(solution)/shard_map/halo_y/pallas_call | solution.py:473
  15.8 6.1 %collective-permute-start.2 = (f32[576,128]{1,0:T(8,128)S(1)}, f32[576,128]{1,0:T(8,128)S(1)}, u32[]{:S(2)}, u32[]{:S(2)}) collective-permute-start(f32[576,128]{1,0:T(8,128)S(1)} %get-tuple-element.45), channel_id=1, source_target_pairs={{0,128},{256,384},{128,0},{384,256},{1,129},{257,385},{129,1},{385... | collective-permute-start | bytes 884744 | tf_op jit(solution)/shard_map/ppermute | solution.py:493
  21.9 1.9 %collective-permute-start.4 = (f32[144,128]{1,0:T(8,128)S(1)}, f32[144,128]{1,0:T(8,128)S(1)}, u32[]{:S(2)}, u32[]{:S(2)}) collective-permute-start(f32[144,128]{1,0:T(8,128)S(1)} %get-tuple-element.47), channel_id=1, source_target_pairs={{128,256},{384,0},{256,128},{0,384},{129,257},{385,1},{257,129},{1... | collective-permute-start | bytes 221192 | tf_op jit(solution)/shard_map/ppermute | solution.py:493
  23.8 3.5 %collective-permute-start.5 = (f32[96,128]{1,0:T(8,128)S(1)}, f32[96,128]{1,0:T(8,128)S(1)}, u32[]{:S(2)}, u32[]{:S(2)}) collective-permute-start(f32[96,128]{1,0:T(8,128)S(1)} %get-tuple-element.51), channel_id=1, source_target_pairs={{0,256},{128,384},{256,0},{384,128},{1,257},{129,385},{257,1},{385... | collective-permute-start | bytes 147464 | tf_op jit(solution)/shard_map/ppermute | solution.py:487
  27.4 1.6 %own_x.1 = (f32[8,256,128]{2,1,0:T(8,128)S(1)}, f32[4,128,128]{2,1,0:T(8,128)S(1)}, f32[2,64,128]{2,1,0:T(8,128)S(1)}) custom-call(f32[8,256,128]{2,1,0:T(8,128)S(1)} %get-tuple-element.35.g1, f32[4,256,128]{2,1,0:T(8,128)S(1)} %get-tuple-element.36.g2, f32[2,256,128]{2,1,0:T(8,128)S(1)} %get-tuple-element.37.g3, f32[3,256,128]{2,1,0:T(8,128)S(1)} %get-tuple-element.42.d_ref), custom_call_target="tpu_custom_call" | custom-call | bytes 8388608 | tf_op jit(solution)/shard_map/own_x/pallas_call | solution.py:473
  28.9 0.0 collective-permute-done.4.refs_4_.refs_3_
  29.0 0.0 collective-permute-done.3.refs_3_.refs_2_
  29.0 0.0 collective-permute-done.2.refs_2_.refs_1_
  29.0 0.5 spill_x.1
  29.5 0.3 collective-permute-done.5.refs_4_
  29.8 0.2 spill_x_last.1
  30.0 1.9 %collective-permute-start.6 = (f32[384,128]{1,0:T(8,128)S(1)}, f32[384,128]{1,0:T(8,128)S(1)}, u32[]{:S(2)}, u32[]{:S(2)}) collective-permute-start(f32[384,128]{1,0:T(8,128)S(1)} %get-tuple-element.57), channel_id=1, source_target_pairs={{0,1},{1,2},{2,3},{3,4},{4,5},{5,6},{6,7},{7,8},{8,9},{9,10},{10,1... | collective-permute-start | bytes 589832 | tf_op jit(solution)/shard_map/ppermute | solution.py:487
  31.9 10.4 %collective-permute-start.7 = (f32[376,128]{1,0:T(8,128)S(1)}, f32[376,128]{1,0:T(8,128)S(1)}, u32[]{:S(2)}, u32[]{:S(2)}) collective-permute-start(f32[376,128]{1,0:T(8,128)S(1)} %get-tuple-element.58), channel_id=1, source_target_pairs={{0,31},{1,0},{2,1},{3,2},{4,3},{5,4},{6,5},{7,6},{8,7},{9,8},{10,9... | collective-permute-start | bytes 577544 | tf_op jit(solution)/shard_map/ppermute | solution.py:487
  42.3 1.9 %collective-permute-start.8 = (f32[16,128]{1,0:T(8,128)S(1)}, f32[16,128]{1,0:T(8,128)S(1)}, u32[]{:S(2)}, u32[]{:S(2)}) collective-permute-start(f32[16,128]{1,0:T(8,128)S(1)} %get-tuple-element.62), channel_id=1, source_target_pairs={{0,2},{1,3},{2,4},{3,5},{4,6},{5,7},{6,8},{7,9},{8,10},{9,11},{10,... | collective-permute-start | bytes 24584 | tf_op jit(solution)/shard_map/ppermute | solution.py:487
  44.3 7.5 %collective-permute-start.9 = (f32[8,128]{1,0:T(8,128)S(1)}, f32[8,128]{1,0:T(8,128)S(1)}, u32[]{:S(2)}, u32[]{:S(2)}) collective-permute-start(f32[8,128]{1,0:T(8,128)S(1)} %get-tuple-element.63), channel_id=1, source_target_pairs={{0,30},{1,31},{2,0},{3,1},{4,2},{5,3},{6,4},{7,5},{8,6},{9,7},{10,... | collective-permute-start | bytes 12296 | tf_op jit(solution)/shard_map/ppermute | solution.py:487
  51.8 0.7 %own_z.1 = (f32[8,16,16,128]{3,2,1,0:T(8,128)S(1)}, f32[4,8,8,128]{3,2,1,0:T(8,128)S(1)}, f32[2,4,4,128]{3,2,1,0:T(4,128)S(1)}) custom-call(f32[8,256,128]{2,1,0:T(8,128)S(1)} %get-tuple-element.48.g1, f32[4,128,128]{2,1,0:T(8,128)S(1)} %get-tuple-element.49.g2, f32[2,64,128]{2,1,0:T(8,128)S(1)} %get-tuple-element.54.g3), custom_call_target="tpu_custom_call" | custom-call | bytes 8388608 | tf_op jit(solution)/shard_map/own_z/pallas_call | solution.py:473
  52.6 0.0 collective-permute-done.7.down_in
  52.6 0.0 collective-permute-done.6.up_in
  52.6 1.0 %spill_z.1 = (f32[7,8,8,512]{3,2,1,0:T(8,128)}, f32[7,4,4,256]{3,2,1,0:T(4,128)}) custom-call(f32[8,16,16,128]{3,2,1,0:T(8,128)S(1)} %get-tuple-element.55.i1, f32[4,8,8,128]{3,2,1,0:T(8,128)S(1)} %get-tuple-element.56.i2, f32[384,128]{1,0:T(8,128)S(1)} %collective-permute-done.6.up_in, f32[376,128]{1,0:T(8,128)S(1)} %collective-permute-done.7.down_in), custom_call_target="tpu_custom_call" | custom-call | bytes 6291456 | tf_op jit(solution)/shard_map/spill_z/pallas_call | solution.py:557
  53.6 0.0 collective-permute-done.9.down2_in
  53.6 0.0 collective-permute-done.8.up2_in
  53.6 0.6 %spill_z_last.1 = (f32[7,2,2,128]{3,2,1,0:T(2,128)}, f32[2,2,128]{2,1,0:T(2,128)}) custom-call(f32[2,4,4,128]{3,2,1,0:T(4,128)S(1)} %get-tuple-element.61.i3, f32[384,128]{1,0:T(8,128)S(1)} %collective-permute-done.6.up_in, f32[376,128]{1,0:T(8,128)S(1)} %collective-permute-done.7.down_in, f32[16,128]{1,0:T(8,128)S(1)} %collective-permute-done.8.up2_in, ...), custom_call_target="tpu_custom_call" | custom-call | bytes 1048576 | tf_op jit(solution)/shard_map/spill_z_last/pallas_call | solution.py:473
Async XLA Ops:
  0.6 8.4 %copy-start = (f32[16,16,1024]{2,1,0:T(8,128)S(1)}, f32[16,16,1024]{2,1,0:T(8,128)}, u32[]{:S(2)}) copy-start(f32[16,16,1024]{2,1,0:T(8,128)} %param.2) | copy-start | bytes 3145732
  1.8 12.3 %collective-permute-start = (f32[64,128]{1,0:T(8,128)S(1)}, f32[64,128]{1,0:T(8,128)S(1)}, u32[]{:S(2)}, u32[]{:S(2)}) collective-permute-start(f32[64,128]{1,0:T(8,128)S(1)} %get-tuple-element.38.first_ref), channel_id=1, source_target_pairs={{0,96},{32,0},{64,32},{96,64},{1,97},{33,1},{65,33},{97,65},{2,98}... | collective-permute-start | bytes 98312 | tf_op jit(solution)/shard_map/ppermute | solution.py:487
  7.1 7.9 %collective-permute-start.1 = (f32[64,128]{1,0:T(8,128)S(1)}, f32[64,128]{1,0:T(8,128)S(1)}, u32[]{:S(2)}, u32[]{:S(2)}) collective-permute-start(f32[64,128]{1,0:T(8,128)S(1)} %get-tuple-element.39.last_ref), channel_id=1, source_target_pairs={{0,32},{32,64},{64,96},{96,0},{1,33},{33,65},{65,97},{97,1},{2,34}... | collective-permute-start | bytes 98312 | tf_op jit(solution)/shard_map/ppermute | solution.py:487
  9.0 6.0 %copy-start.1 = (f32[128,384]{1,0:T(8,128)S(1)}, f32[128,384]{1,0:T(8,128)}, u32[]{:S(2)}) copy-start(f32[128,384]{1,0:T(8,128)} %constant.21.clone.w_ref) | copy-start | bytes 589828
  11.7 17.2 %collective-permute-start.3 = (f32[576,128]{1,0:T(8,128)S(1)}, f32[576,128]{1,0:T(8,128)S(1)}, u32[]{:S(2)}, u32[]{:S(2)}) collective-permute-start(f32[576,128]{1,0:T(8,128)S(1)} %get-tuple-element.46), channel_id=1, source_target_pairs={{128,256},{384,0},{256,128},{0,384},{129,257},{385,1},{257,129},{1... | collective-permute-start | bytes 884744 | tf_op jit(solution)/shard_map/ppermute | solution.py:493
  15.8 13.1 %collective-permute-start.2 = (f32[576,128]{1,0:T(8,128)S(1)}, f32[576,128]{1,0:T(8,128)S(1)}, u32[]{:S(2)}, u32[]{:S(2)}) collective-permute-start(f32[576,128]{1,0:T(8,128)S(1)} %get-tuple-element.45), channel_id=1, source_target_pairs={{0,128},{256,384},{128,0},{384,256},{1,129},{257,385},{129,1},{385... | collective-permute-start | bytes 884744 | tf_op jit(solution)/shard_map/ppermute | solution.py:493
  21.9 7.1 %collective-permute-start.4 = (f32[144,128]{1,0:T(8,128)S(1)}, f32[144,128]{1,0:T(8,128)S(1)}, u32[]{:S(2)}, u32[]{:S(2)}) collective-permute-start(f32[144,128]{1,0:T(8,128)S(1)} %get-tuple-element.47), channel_id=1, source_target_pairs={{128,256},{384,0},{256,128},{0,384},{129,257},{385,1},{257,129},{1... | collective-permute-start | bytes 221192 | tf_op jit(solution)/shard_map/ppermute | solution.py:493
  23.8 6.0 %collective-permute-start.5 = (f32[96,128]{1,0:T(8,128)S(1)}, f32[96,128]{1,0:T(8,128)S(1)}, u32[]{:S(2)}, u32[]{:S(2)}) collective-permute-start(f32[96,128]{1,0:T(8,128)S(1)} %get-tuple-element.51), channel_id=1, source_target_pairs={{0,256},{128,384},{256,0},{384,128},{1,257},{129,385},{257,1},{385... | collective-permute-start | bytes 147464 | tf_op jit(solution)/shard_map/ppermute | solution.py:487
  30.0 22.6 %collective-permute-start.6 = (f32[384,128]{1,0:T(8,128)S(1)}, f32[384,128]{1,0:T(8,128)S(1)}, u32[]{:S(2)}, u32[]{:S(2)}) collective-permute-start(f32[384,128]{1,0:T(8,128)S(1)} %get-tuple-element.57), channel_id=1, source_target_pairs={{0,1},{1,2},{2,3},{3,4},{4,5},{5,6},{6,7},{7,8},{8,9},{9,10},{10,1... | collective-permute-start | bytes 589832 | tf_op jit(solution)/shard_map/ppermute | solution.py:487
  31.9 20.7 %collective-permute-start.7 = (f32[376,128]{1,0:T(8,128)S(1)}, f32[376,128]{1,0:T(8,128)S(1)}, u32[]{:S(2)}, u32[]{:S(2)}) collective-permute-start(f32[376,128]{1,0:T(8,128)S(1)} %get-tuple-element.58), channel_id=1, source_target_pairs={{0,31},{1,0},{2,1},{3,2},{4,3},{5,4},{6,5},{7,6},{8,7},{9,8},{10,9... | collective-permute-start | bytes 577544 | tf_op jit(solution)/shard_map/ppermute | solution.py:487
  42.3 11.3 %collective-permute-start.8 = (f32[16,128]{1,0:T(8,128)S(1)}, f32[16,128]{1,0:T(8,128)S(1)}, u32[]{:S(2)}, u32[]{:S(2)}) collective-permute-start(f32[16,128]{1,0:T(8,128)S(1)} %get-tuple-element.62), channel_id=1, source_target_pairs={{0,2},{1,3},{2,4},{3,5},{4,6},{5,7},{6,8},{7,9},{8,10},{9,11},{10,... | collective-permute-start | bytes 24584 | tf_op jit(solution)/shard_map/ppermute | solution.py:487
  44.3 9.3 %collective-permute-start.9 = (f32[8,128]{1,0:T(8,128)S(1)}, f32[8,128]{1,0:T(8,128)S(1)}, u32[]{:S(2)}, u32[]{:S(2)}) collective-permute-start(f32[8,128]{1,0:T(8,128)S(1)} %get-tuple-element.63), channel_id=1, source_target_pairs={{0,30},{1,31},{2,0},{3,1},{4,2},{5,3},{6,4},{7,5},{8,6},{9,7},{10,... | collective-permute-start | bytes 12296 | tf_op jit(solution)/shard_map/ppermute | solution.py:487

commit v5 on v4

--- a/solution.py
+++ b/solution.py
@@ -150,19 +150,17 @@
 Z_DOWN2 = message_places(Z_HEIGHT, (-2,), (3,))
 
 
-def pack_kernel(first_ref, last_ref, to_down_ref, to_up_ref):
+def pack_kernel(turn, x_ref, out_ref):
     lane = lax.broadcasted_iota(jnp.int32, (64, 128), 1)
-    down = up = jnp.zeros((64, 128), F32)
+    packed = jnp.zeros((64, 128), F32)
     for g in range(4):
         mine = (lane >= 32 * g) & (lane < 32 * g + 32)
-        rows = pl.ds(64 * g, 64)
-        a, b = first_ref[rows, :], last_ref[rows, :]
-        a = pltpu.roll(a, 32 * g, 1) if g else a
-        b = pltpu.roll(b, (32 * g + 32) % 128, 1) if (32 * g + 32) % 128 else b
-        down = jnp.where(mine, a, down)
-        up = jnp.where(mine, b, up)
-    to_down_ref[...] = down
-    to_up_ref[...] = up
+        a = x_ref[pl.ds(64 * g, 64), pl.ds(0 if turn == 0 else x_ref.shape[1] - 128, 128)]
+        by = (32 * g + turn) % 128
+        packed = jnp.where(mine, pltpu.roll(a, by, 1) if by else a, packed)
+    out_ref[:64, :] = packed
+    if out_ref.shape[0] > 64:
+        out_ref[64:, :] = jnp.zeros((out_ref.shape[0] - 64, 128), F32)
 
 
 def split_dot(x, selection):
@@ -186,8 +184,8 @@
             both = split_dot(source(t, rows), pick)
             even[rows, pl.ds(128 * t, 128)] = both[:, :128]
             odd[rows, pl.ds(128 * t, 128)] = both[:, 128:]
-        for r in range(block, block + 128, 16):
-            rows = pl.ds(r, 16)
+        for r in range(block, block + 128, 64):
+            rows = pl.ds(r, 64)
             s, d = even[rows, :width], odd[rows, :width]
             ahead = lambda v: pltpu.roll(v, width - 1, 1)
             behind = lambda v: pltpu.roll(v, 1, 1)
@@ -290,7 +288,7 @@
 ):
     lane = lax.broadcasted_iota(jnp.int32, (64, 128), 1)
     for g in range(4):
-        a, b = above_ref[...] - first_ref[...], below_ref[...] - last_ref[...]
+        a, b = above_ref[...] - first_ref[...], below_ref[:64, :] - last_ref[:64, :]
         a = pltpu.roll(a, 128 - 32 * g, 1) if g else a
         b = pltpu.roll(b, 96 - 32 * g, 1) if g < 3 else b
         halo[pl.ds(64 * g, 64), :] = jnp.where(lane < 32, a, jnp.where(lane >= 96, b, 0.0))
@@ -496,15 +494,16 @@
 def on_device(density):
     flat = density.reshape(N * N, 1024)
     in_hbm = pinned([flat], pltpu.HBM)[0]
-    to_down, to_up = pl.pallas_call(
-        pack_kernel,
+    (to_up,) = pl.pallas_call(
+        functools.partial(pack_kernel, 32),
         grid=(1,),
-        out_shape=in_vmem((64, 128), (64, 128)),
-        in_specs=[pl.BlockSpec((256, 128), lambda i: (0, 0)), pl.BlockSpec((256, 128), lambda i: (0, 7))],
-        out_specs=(VMEM, VMEM),
+        out_shape=in_vmem((72, 128)),
+        in_specs=[pl.BlockSpec((256, 128), lambda i: (0, 7))],
+        out_specs=(VMEM,),
         compiler_params=PARAMS,
-        name="pack_y",
-    )(in_hbm, in_hbm)
+        name="pack_up",
+    )(in_hbm)
+    (to_down,) = call(functools.partial(pack_kernel, 0), (flat,), in_vmem((64, 128)), "pack_down", (), 1)
     above = shift(to_down, "gy", -1)
     below = shift(to_up, "gy", 1)
 

time: 54.6 us -> 54.5 us (level)
  the two profiles are of different devices: /device:TPU:8 before, /device:TPU:24 now
where the time goes in v5:
time: 54.5 us; the launch traced here: 54.2 us
  starting transfers between devices  42.8 us (79%)
  Pallas kernels  9.25 us (17%)
  waiting for transfers between devices  1.21 us (2%)
  between operations  0.85 us (2%)
    ppermute x7, starting transfers between devices, shift(): return lax.ppermute(x, axis, [(i, (i + by) % peers) for i in range(peers)])  34.6 us
    ppermute x3, starting transfers between devices, swap(): return lax.ppermute(x, axis, pairs + [(b, a) for a, b in pairs])  8.24 us
    pallas_call x8, Pallas kernels, call(): pl.pallas_call(kernel, out_shape=out_shape, in_specs=specs, out_specs=tup...  7.16 us
    ppermute x7, waiting for transfers between devices, shift(): return lax.ppermute(x, axis, [(i, (i + by) % peers) for i in range(peers)])  1.2 us
  transfers between devices with their start and end apart: 10, of which 2 were waited for; matrix products, arithmetic and copies ran while one was open for 0% of the time, Pallas kernels for 14%

profile of v5, /device:TPU:24, one launch (start us, length us, event | category | flops | bytes accessed | tf_op | source)
XLA Modules:
  0.0 54.2 jit_solution(3930793311278384330)
XLA Ops:
  0.6 0.0 copy-start
  0.6 1.1 %pack_up.1.last_ref = f32[72,128]{1,0:T(8,128)S(1)} custom-call(f32[256,1024]{1,0:T(8,128)} %bitcast.2), custom_call_target="tpu_custom_call" | custom-call | tf_op jit(solution)/shard_map/pack_up/pallas_call | solution.py:497
  1.7 4.8 %collective-permute-start.1 = (f32[72,128]{1,0:T(8,128)S(1)}, f32[72,128]{1,0:T(8,128)S(1)}, u32[]{:S(2)}, u32[]{:S(2)}) collective-permute-start(f32[72,128]{1,0:T(8,128)S(1)} %pack_up.1.last_ref), channel_id=1, source_target_pairs={{0,32},{32,64},{64,96},{96,0},{1,33},{33,65},{65,97},{97,1},{2,34}... | collective-permute-start | bytes 110600 | tf_op jit(solution)/shard_map/ppermute | solution.py:485
  6.5 0.0 copy-done
  6.6 0.1 pack_down.1.first_ref
  6.7 1.9 %collective-permute-start = (f32[64,128]{1,0:T(8,128)S(1)}, f32[64,128]{1,0:T(8,128)S(1)}, u32[]{:S(2)}, u32[]{:S(2)}) collective-permute-start(f32[64,128]{1,0:T(8,128)S(1)} %pack_down.1.first_ref), channel_id=1, source_target_pairs={{0,96},{32,0},{64,32},{96,64},{1,97},{33,1},{65,33},{97,65},{2,98}... | collective-permute-start | bytes 98312 | tf_op jit(solution)/shard_map/ppermute | solution.py:485
  8.6 0.0 copy-start.1
  8.6 2.7 %own_y.1 = (f32[8,256,128]{2,1,0:T(8,128)S(1)}, f32[4,256,128]{2,1,0:T(8,128)S(1)}, f32[2,256,128]{2,1,0:T(8,128)S(1)}, f32[576,128]{1,0:T(8,128)S(1)}, f32[576,128]{1,0:T(8,128)S(1)}, /*index=5*/f32[96,128]{1,0:T(8,128)S(1)}) custom-call(s32[1]{0:T(128)} %bitcast.odd_ref, f32[256,1024]{1,0:T(8,128)S(1)} %bitcast.4), custom_call_target="tpu_custom_call" | custom-call | bytes 12582912 | tf_op jit(solution)/shard_map/own_y/pallas_call | solution.py:471
  11.3 2.4 %collective-permute-start.3 = (f32[576,128]{1,0:T(8,128)S(1)}, f32[576,128]{1,0:T(8,128)S(1)}, u32[]{:S(2)}, u32[]{:S(2)}) collective-permute-start(f32[576,128]{1,0:T(8,128)S(1)} %get-tuple-element.42), channel_id=1, source_target_pairs={{128,256},{384,0},{256,128},{0,384},{129,257},{385,1},{257,129},{1... | collective-permute-start | bytes 884744 | tf_op jit(solution)/shard_map/ppermute | solution.py:491
  13.7 0.9 %collective-permute-done.above_ref = f32[64,128]{1,0:T(8,128)S(1)} collective-permute-done((f32[64,128]{1,0:T(8,128)S(1)}, f32[64,128]{1,0:T(8,128)S(1)}, u32[]{:S(2)}, u32[]{:S(2)}) %collective-permute-start) | collective-permute-done | bytes 32800 | tf_op jit(solution)/shard_map/ppermute | solution.py:485
  14.6 0.0 collective-permute-done.1.below_ref
  14.6 0.0 copy-done.1
  14.6 0.8 %halo_y.1 = (f32[3,256,128]{2,1,0:T(8,128)S(1)}, f32[576,128]{1,0:T(8,128)S(1)}, f32[144,128]{1,0:T(8,128)S(1)}, f32[96,128]{1,0:T(8,128)S(1)}) custom-call(s32[1]{0:T(128)} %bitcast.odd_ref, f32[64,128]{1,0:T(8,128)S(1)} %collective-permute-done.above_ref, f32[72,128]{1,0:T(8,128)S(1)} %collective-permute-done.1.below_ref, ...), custom_call_target="tpu_custom_call" | custom-call | bytes 4194304 | tf_op jit(solution)/shard_map/halo_y/pallas_call | solution.py:471
  15.4 3.9 %collective-permute-start.2 = (f32[576,128]{1,0:T(8,128)S(1)}, f32[576,128]{1,0:T(8,128)S(1)}, u32[]{:S(2)}, u32[]{:S(2)}) collective-permute-start(f32[576,128]{1,0:T(8,128)S(1)} %get-tuple-element.41), channel_id=1, source_target_pairs={{0,128},{256,384},{128,0},{384,256},{1,129},{257,385},{129,1},{385... | collective-permute-start | bytes 884744 | tf_op jit(solution)/shard_map/ppermute | solution.py:491
  19.3 1.9 %collective-permute-start.4 = (f32[144,128]{1,0:T(8,128)S(1)}, f32[144,128]{1,0:T(8,128)S(1)}, u32[]{:S(2)}, u32[]{:S(2)}) collective-permute-start(f32[144,128]{1,0:T(8,128)S(1)} %get-tuple-element.43), channel_id=1, source_target_pairs={{128,256},{384,0},{256,128},{0,384},{129,257},{385,1},{257,129},{1... | collective-permute-start | bytes 221192 | tf_op jit(solution)/shard_map/ppermute | solution.py:491
  21.2 3.5 %collective-permute-start.5 = (f32[96,128]{1,0:T(8,128)S(1)}, f32[96,128]{1,0:T(8,128)S(1)}, u32[]{:S(2)}, u32[]{:S(2)}) collective-permute-start(f32[96,128]{1,0:T(8,128)S(1)} %get-tuple-element.47), channel_id=1, source_target_pairs={{0,256},{128,384},{256,0},{384,128},{1,257},{129,385},{257,1},{385... | collective-permute-start | bytes 147464 | tf_op jit(solution)/shard_map/ppermute | solution.py:485
  24.8 1.6 %own_x.1 = (f32[8,256,128]{2,1,0:T(8,128)S(1)}, f32[4,128,128]{2,1,0:T(8,128)S(1)}, f32[2,64,128]{2,1,0:T(8,128)S(1)}) custom-call(f32[8,256,128]{2,1,0:T(8,128)S(1)} %get-tuple-element.33.g1, f32[4,256,128]{2,1,0:T(8,128)S(1)} %get-tuple-element.34.g2, f32[2,256,128]{2,1,0:T(8,128)S(1)} %get-tuple-element.35.g3, f32[3,256,128]{2,1,0:T(8,128)S(1)} %get-tuple-element.38.d_ref), custom_call_target="tpu_custom_call" | custom-call | bytes 8388608 | tf_op jit(solution)/shard_map/own_x/pallas_call | solution.py:471
  26.4 0.0 collective-permute-done.4.refs_4_.refs_3_
  26.4 0.0 collective-permute-done.3.refs_3_.refs_2_
  26.4 0.0 collective-permute-done.2.refs_2_.refs_1_
  26.4 0.5 spill_x.1
  26.9 0.3 collective-permute-done.5.refs_4_
  27.2 0.2 spill_x_last.1
  27.4 3.2 %collective-permute-start.6 = (f32[384,128]{1,0:T(8,128)S(1)}, f32[384,128]{1,0:T(8,128)S(1)}, u32[]{:S(2)}, u32[]{:S(2)}) collective-permute-start(f32[384,128]{1,0:T(8,128)S(1)} %get-tuple-element.53), channel_id=1, source_target_pairs={{0,1},{1,2},{2,3},{3,4},{4,5},{5,6},{6,7},{7,8},{8,9},{9,10},{10,1... | collective-permute-start | bytes 589832 | tf_op jit(solution)/shard_map/ppermute | solution.py:485
  30.6 11.7 %collective-permute-start.7 = (f32[376,128]{1,0:T(8,128)S(1)}, f32[376,128]{1,0:T(8,128)S(1)}, u32[]{:S(2)}, u32[]{:S(2)}) collective-permute-start(f32[376,128]{1,0:T(8,128)S(1)} %get-tuple-element.54), channel_id=1, source_target_pairs={{0,31},{1,0},{2,1},{3,2},{4,3},{5,4},{6,5},{7,6},{8,7},{9,8},{10,9... | collective-permute-start | bytes 577544 | tf_op jit(solution)/shard_map/ppermute | solution.py:485
  42.3 1.9 %collective-permute-start.8 = (f32[16,128]{1,0:T(8,128)S(1)}, f32[16,128]{1,0:T(8,128)S(1)}, u32[]{:S(2)}, u32[]{:S(2)}) collective-permute-start(f32[16,128]{1,0:T(8,128)S(1)} %get-tuple-element.58), channel_id=1, source_target_pairs={{0,2},{1,3},{2,4},{3,5},{4,6},{5,7},{6,8},{7,9},{8,10},{9,11},{10,... | collective-permute-start | bytes 24584 | tf_op jit(solution)/shard_map/ppermute | solution.py:485
  44.2 7.5 %collective-permute-start.9 = (f32[8,128]{1,0:T(8,128)S(1)}, f32[8,128]{1,0:T(8,128)S(1)}, u32[]{:S(2)}, u32[]{:S(2)}) collective-permute-start(f32[8,128]{1,0:T(8,128)S(1)} %get-tuple-element.59), channel_id=1, source_target_pairs={{0,30},{1,31},{2,0},{3,1},{4,2},{5,3},{6,4},{7,5},{8,6},{9,7},{10,... | collective-permute-start | bytes 12296 | tf_op jit(solution)/shard_map/ppermute | solution.py:485
  51.7 0.7 %own_z.1 = (f32[8,16,16,128]{3,2,1,0:T(8,128)S(1)}, f32[4,8,8,128]{3,2,1,0:T(8,128)S(1)}, f32[2,4,4,128]{3,2,1,0:T(4,128)S(1)}) custom-call(f32[8,256,128]{2,1,0:T(8,128)S(1)} %get-tuple-element.44.g1, f32[4,128,128]{2,1,0:T(8,128)S(1)} %get-tuple-element.45.g2, f32[2,64,128]{2,1,0:T(8,128)S(1)} %get-tuple-element.50.g3), custom_call_target="tpu_custom_call" | custom-call | bytes 8388608 | tf_op jit(solution)/shard_map/own_z/pallas_call | solution.py:471
  52.5 0.0 collective-permute-done.7.down_in
  52.5 0.0 collective-permute-done.6.up_in
  52.5 1.0 %spill_z.1 = (f32[7,8,8,512]{3,2,1,0:T(8,128)}, f32[7,4,4,256]{3,2,1,0:T(4,128)}) custom-call(f32[8,16,16,128]{3,2,1,0:T(8,128)S(1)} %get-tuple-element.51.i1, f32[4,8,8,128]{3,2,1,0:T(8,128)S(1)} %get-tuple-element.52.i2, f32[384,128]{1,0:T(8,128)S(1)} %collective-permute-done.6.up_in, f32[376,128]{1,0:T(8,128)S(1)} %collective-permute-done.7.down_in), custom_call_target="tpu_custom_call" | custom-call | bytes 6291456 | tf_op jit(solution)/shard_map/spill_z/pallas_call | solution.py:556
  53.5 0.0 collective-permute-done.9.down2_in
  53.5 0.0 collective-permute-done.8.up2_in
  53.5 0.6 %spill_z_last.1 = (f32[7,2,2,128]{3,2,1,0:T(2,128)}, f32[2,2,128]{2,1,0:T(2,128)}) custom-call(f32[2,4,4,128]{3,2,1,0:T(4,128)S(1)} %get-tuple-element.57.i3, f32[384,128]{1,0:T(8,128)S(1)} %collective-permute-done.6.up_in, f32[376,128]{1,0:T(8,128)S(1)} %collective-permute-done.7.down_in, f32[16,128]{1,0:T(8,128)S(1)} %collective-permute-done.8.up2_in, ...), custom_call_target="tpu_custom_call" | custom-call | bytes 1048576 | tf_op jit(solution)/shard_map/spill_z_last/pallas_call | solution.py:471
Async XLA Ops:
  0.6 5.9 %copy-start = (f32[16,16,1024]{2,1,0:T(8,128)S(1)}, f32[16,16,1024]{2,1,0:T(8,128)}, u32[]{:S(2)}) copy-start(f32[16,16,1024]{2,1,0:T(8,128)} %param.2) | copy-start | bytes 3145732
  1.7 12.8 %collective-permute-start.1 = (f32[72,128]{1,0:T(8,128)S(1)}, f32[72,128]{1,0:T(8,128)S(1)}, u32[]{:S(2)}, u32[]{:S(2)}) collective-permute-start(f32[72,128]{1,0:T(8,128)S(1)} %pack_up.1.last_ref), channel_id=1, source_target_pairs={{0,32},{32,64},{64,96},{96,0},{1,33},{33,65},{65,97},{97,1},{2,34}... | collective-permute-start | bytes 110600 | tf_op jit(solution)/shard_map/ppermute | solution.py:485
  6.7 7.9 %collective-permute-start = (f32[64,128]{1,0:T(8,128)S(1)}, f32[64,128]{1,0:T(8,128)S(1)}, u32[]{:S(2)}, u32[]{:S(2)}) collective-permute-start(f32[64,128]{1,0:T(8,128)S(1)} %pack_down.1.first_ref), channel_id=1, source_target_pairs={{0,96},{32,0},{64,32},{96,64},{1,97},{33,1},{65,33},{97,65},{2,98}... | collective-permute-start | bytes 98312 | tf_op jit(solution)/shard_map/ppermute | solution.py:485
  8.6 6.0 %copy-start.1 = (f32[128,384]{1,0:T(8,128)S(1)}, f32[128,384]{1,0:T(8,128)}, u32[]{:S(2)}) copy-start(f32[128,384]{1,0:T(8,128)} %constant.21.clone.w_ref) | copy-start | bytes 589828
  11.3 15.1 %collective-permute-start.3 = (f32[576,128]{1,0:T(8,128)S(1)}, f32[576,128]{1,0:T(8,128)S(1)}, u32[]{:S(2)}, u32[]{:S(2)}) collective-permute-start(f32[576,128]{1,0:T(8,128)S(1)} %get-tuple-element.42), channel_id=1, source_target_pairs={{128,256},{384,0},{256,128},{0,384},{129,257},{385,1},{257,129},{1... | collective-permute-start | bytes 884744 | tf_op jit(solution)/shard_map/ppermute | solution.py:491
  15.4 11.0 %collective-permute-start.2 = (f32[576,128]{1,0:T(8,128)S(1)}, f32[576,128]{1,0:T(8,128)S(1)}, u32[]{:S(2)}, u32[]{:S(2)}) collective-permute-start(f32[576,128]{1,0:T(8,128)S(1)} %get-tuple-element.41), channel_id=1, source_target_pairs={{0,128},{256,384},{128,0},{384,256},{1,129},{257,385},{129,1},{385... | collective-permute-start | bytes 884744 | tf_op jit(solution)/shard_map/ppermute | solution.py:491
  19.3 7.1 %collective-permute-start.4 = (f32[144,128]{1,0:T(8,128)S(1)}, f32[144,128]{1,0:T(8,128)S(1)}, u32[]{:S(2)}, u32[]{:S(2)}) collective-permute-start(f32[144,128]{1,0:T(8,128)S(1)} %get-tuple-element.43), channel_id=1, source_target_pairs={{128,256},{384,0},{256,128},{0,384},{129,257},{385,1},{257,129},{1... | collective-permute-start | bytes 221192 | tf_op jit(solution)/shard_map/ppermute | solution.py:491
  21.2 6.0 %collective-permute-start.5 = (f32[96,128]{1,0:T(8,128)S(1)}, f32[96,128]{1,0:T(8,128)S(1)}, u32[]{:S(2)}, u32[]{:S(2)}) collective-permute-start(f32[96,128]{1,0:T(8,128)S(1)} %get-tuple-element.47), channel_id=1, source_target_pairs={{0,256},{128,384},{256,0},{384,128},{1,257},{129,385},{257,1},{385... | collective-permute-start | bytes 147464 | tf_op jit(solution)/shard_map/ppermute | solution.py:485
  27.4 25.1 %collective-permute-start.6 = (f32[384,128]{1,0:T(8,128)S(1)}, f32[384,128]{1,0:T(8,128)S(1)}, u32[]{:S(2)}, u32[]{:S(2)}) collective-permute-start(f32[384,128]{1,0:T(8,128)S(1)} %get-tuple-element.53), channel_id=1, source_target_pairs={{0,1},{1,2},{2,3},{3,4},{4,5},{5,6},{6,7},{7,8},{8,9},{9,10},{10,1... | collective-permute-start | bytes 589832 | tf_op jit(solution)/shard_map/ppermute | solution.py:485
  30.6 21.9 %collective-permute-start.7 = (f32[376,128]{1,0:T(8,128)S(1)}, f32[376,128]{1,0:T(8,128)S(1)}, u32[]{:S(2)}, u32[]{:S(2)}) collective-permute-start(f32[376,128]{1,0:T(8,128)S(1)} %get-tuple-element.54), channel_id=1, source_target_pairs={{0,31},{1,0},{2,1},{3,2},{4,3},{5,4},{6,5},{7,6},{8,7},{9,8},{10,9... | collective-permute-start | bytes 577544 | tf_op jit(solution)/shard_map/ppermute | solution.py:485
  42.3 11.3 %collective-permute-start.8 = (f32[16,128]{1,0:T(8,128)S(1)}, f32[16,128]{1,0:T(8,128)S(1)}, u32[]{:S(2)}, u32[]{:S(2)}) collective-permute-start(f32[16,128]{1,0:T(8,128)S(1)} %get-tuple-element.58), channel_id=1, source_target_pairs={{0,2},{1,3},{2,4},{3,5},{4,6},{5,7},{6,8},{7,9},{8,10},{9,11},{10,... | collective-permute-start | bytes 24584 | tf_op jit(solution)/shard_map/ppermute | solution.py:485
  44.2 9.3 %collective-permute-start.9 = (f32[8,128]{1,0:T(8,128)S(1)}, f32[8,128]{1,0:T(8,128)S(1)}, u32[]{:S(2)}, u32[]{:S(2)}) collective-permute-start(f32[8,128]{1,0:T(8,128)S(1)} %get-tuple-element.59), channel_id=1, source_target_pairs={{0,30},{1,31},{2,0},{3,1},{4,2},{5,3},{6,4},{7,5},{8,6},{9,7},{10,... | collective-permute-start | bytes 12296 | tf_op jit(solution)/shard_map/ppermute | solution.py:485
